TPU v7x, 256 devices: a whole 4x4x8 slice. The times are simulated.
256 devices in a mesh: lat: 32 (over z, x_hi, core), lon: 8 (over x_lo, y).
Axes of the slice: x: 4 (x_hi: 2, x_lo: 2; x = x_hi * 2 + x_lo), y: 4, z: 8, core: 2. Of those that a mesh axis runs over, the one named last changes fastest.
Arguments:
- kept_modes: bfloat16 [64, 90, 2, 768], P('lat', None, None, 'lon'), may hold values from -6 to 6
- decoder_weight: bfloat16 [768, 1280], replicated, may hold values from -0.21875 to 0.21875
- conv_in_weight: bfloat16 [3, 3, 20, 256], replicated, may hold values from -0.4375 to 0.4375
- conv_mid_weight: bfloat16 [3, 3, 256, 256], replicated, may hold values from -0.125 to 0.125
- conv_out_weight: bfloat16 [3, 3, 256, 1], replicated, may hold values from -0.125 to 0.125
Outputs:
- precipitation: float32 [512, 1440], P('lat', 'lon')
All inputs are finite; a program needn't handle non-finite values.
Results may differ from a plain program's by a relative error of at most 0.025.
Values may be sent and summed in bfloat16 or wider, within the bound.
A program may use at most 128 MiB of HBM per device.

v0:
```python
import math

import jax
import jax.numpy as jnp
from jax import lax
from jax.sharding import PartitionSpec as P

LON_TOK = 180
PATCH = 8


def padded_2(block, sides, width):
    for axis, dim in sides:
        count = lax.axis_size(axis)
        forward = [(i, i + 1) for i in range(count - 1)]
        forward.append((count - 1, 0))
        backward = [(target, source) for source, target in forward]
        low = lax.ppermute(
            lax.slice_in_dim(block, block.shape[dim] - width, None, axis=dim), axis, forward
        )
        high = lax.ppermute(lax.slice_in_dim(block, 0, width, axis=dim), axis, backward)
        block = jnp.concatenate([low, block, high], axis=dim)
    return block


def spectral_table(token_ids, mode_count, length):
    mode_ids = jnp.arange(mode_count, dtype=jnp.int32)
    turns = token_ids[:, None] * mode_ids[None, :] % length
    phase_angle = turns.astype(jnp.float32) * (2.0 * math.pi / length)
    scaling = jnp.where(mode_ids == 0, 1.0, 2.0).astype(jnp.float32) / math.sqrt(length)
    dft_table = jnp.stack([scaling * jnp.cos(phase_angle), -scaling * jnp.sin(phase_angle)], axis=2)
    return dft_table.reshape(token_ids.shape[0], 2 * mode_count)


def window_table(first_token, count, mode_count):
    token_ids = (first_token + jnp.arange(count, dtype=jnp.int32)) % LON_TOK
    return spectral_table(token_ids, mode_count, LON_TOK)


def synthesize(modes, table):
    token_rows = modes.shape[0]
    mode_count = modes.shape[1]
    chan_count = modes.shape[3]
    flat = modes.astype(jnp.float32).reshape(token_rows, 2 * mode_count, chan_count)
    return jnp.einsum("jq,tqc->tjc", table, flat, precision=lax.Precision.HIGHEST).astype(
        jnp.bfloat16
    )


def decode_rows(field, weight_rows, offset, col_count):
    chan_count = field.shape[2]
    shaped = weight_rows.reshape(chan_count, PATCH, PATCH, weight_rows.shape[1] // (PATCH * PATCH))
    block = jnp.einsum("tjc,cabo->otajb", field, shaped, preferred_element_type=jnp.float32)
    block = block.reshape(block.shape[0], field.shape[0] * PATCH, field.shape[1] * PATCH)
    return lax.dynamic_slice_in_dim(block, offset, col_count, 2)


def conv_channels_first(x, weight):
    row_count = x.shape[1] - 2
    col_count = x.shape[2] - 2
    running = jnp.zeros((row_count, col_count, weight.shape[3]), jnp.float32)
    for row_off in range(3):
        for col_off in range(3):
            window = x[:, row_off : row_off + row_count, col_off : col_off + col_count]
            running = running + jnp.einsum(
                "irc,io->rco", window, weight[row_off, col_off], preferred_element_type=jnp.float32
            )
    return running


def conv_valid(x, weight):
    row_count = x.shape[0] - 2
    col_count = x.shape[1] - 2
    running = jnp.zeros((row_count, col_count, weight.shape[3]), jnp.float32)
    for row_off in range(3):
        for col_off in range(3):
            window = x[row_off : row_off + row_count, col_off : col_off + col_count]
            running = running + jnp.einsum(
                "rci,io->rco", window, weight[row_off, col_off], preferred_element_type=jnp.float32
            )
    return running


def conv_single(x, weight):
    row_count = x.shape[0] - 2
    col_count = x.shape[1] - 2
    running = jnp.zeros((row_count, col_count), jnp.float32)
    for row_off in range(3):
        for col_off in range(3):
            window = x[row_off : row_off + row_count, col_off : col_off + col_count]
            running = running + jnp.einsum(
                "rci,i->rc",
                window,
                weight[row_off, col_off, :, 0],
                preferred_element_type=jnp.float32,
            )
    return running


def zero_rim(x, rim, axis):
    count = x.shape[axis]
    lat_index = lax.axis_index("lat")
    last_index = lax.axis_size("lat") - 1
    row_ids = jnp.arange(count, dtype=jnp.int32)
    dropped = (row_ids < rim) & (lat_index == 0) | (row_ids >= count - rim) & (
        lat_index == last_index
    )
    mask_shape = [1] * x.ndim
    mask_shape[axis] = count
    return jnp.where(dropped.reshape(mask_shape), jnp.zeros_like(x), x)


def pad_hidden(hidden):
    padded = padded_2(hidden, (("lat", 0), ("lon", 1)), 1)
    return zero_rim(padded, 1, 0)


def per_device(kept_modes, decoder_weight, conv_in_weight, conv_mid_weight, conv_out_weight):
    mode_count = kept_modes.shape[1]
    width_dev = LON_TOK * PATCH // lax.axis_size("lon")
    lon_index = lax.axis_index("lon")
    col_first = lon_index * width_dev
    first_token = col_first // PATCH
    table = window_table(first_token, width_dev // PATCH + 2, mode_count)
    offset = col_first - first_token * PATCH
    field = synthesize(lax.all_gather(kept_modes, "lon", axis=3, tiled=True), table)
    pixels = decode_rows(field, decoder_weight, offset, width_dev).astype(jnp.bfloat16)
    padded = padded_2(pixels, (("lat", 1), ("lon", 2)), 1)
    padded = zero_rim(padded, 1, 1)
    first = jnp.maximum(conv_channels_first(padded, conv_in_weight), 0.0).astype(jnp.bfloat16)
    second = jnp.maximum(conv_valid(pad_hidden(first), conv_mid_weight), 0.0).astype(jnp.bfloat16)
    output = conv_single(pad_hidden(second), conv_out_weight)
    return output


def solution(mesh):
    placed = (P("lat", None, None, "lon"), P(), P(), P(), P())
    return jax.shard_map(
        per_device, mesh=mesh, in_specs=placed, out_specs=P("lat", "lon"), check_vma=False
    )
```

profile of v0, /device:TPU:103, one launch (start us, length us, event | category | flops | bytes accessed | tf_op | source)
XLA Modules:
  0.0 114.4 jit_solution(7044258527500154538)
XLA Ops:
  0.0 1.0 copy.10
  1.1 23.7 %all_gather.3 = bf16[2,90,2,768]{1,2,0,3:T(2,128)(2,1)S(1)} all-gather(bf16[2,90,2,96]{1,2,0,3:T(2,128)(2,1)S(1)} %copy.10), channel_id=1, replica_groups=mesh['lat'=32,'lon'=8] {'lon'}, dimensions={3}, use_global_device_ids=true | all-gather | bytes 622080 | tf_op jit(solution)/shard_map/all_gather | solution.py:126
  24.8 2.7 %copy.12 = bf16[768,1280]{0,1:T(8,128)(2,1)S(1)} copy(bf16[768,1280]{1,0:T(8,128)(2,1)} %param.6) | data formatting | bytes 3932160 | tf_op args[1]
  27.4 2.1 %reshape.181 = bf16[768,8,8,20,1]{0,3,2,1,4:T(8,128)(2,1)} reshape(bf16[768,1280]{0,1:T(8,128)(2,1)S(1)} %copy.12) | data formatting | bytes 3932160 | tf_op jit(solution)/shard_map/reshape | solution.py:52
  30.4 4.0 %convolution_bitcast_fusion = bf16[20,2,8,24,8]{0,3,4,2,1:T(8,128)(2,1)S(1)} fusion(bf16[2,24,768,1,1]{2,1,4,3,0:T(8,128)(2,1)S(1)} %fusion.36, bf16[768,8,8,20,1]{0,3,2,1,4:T(8,128)(2,1)} %reshape.181), kind=kOutput, calls=%fused_computation.39 | convolution fusion | flops 94371840 | bytes 2162688 | tf_op jit(solution)/shard_map/tjc,cabo->otajb/dot_general | solution.py:53
  35.2 10.4 %collective-permute-start = (bf16[20,1,180]{2,0,1:T(8,128)(2,1)S(1)}, bf16[20,1,180]{2,0,1:T(8,128)(2,1)S(1)}, u32[]{:S(2)}, u32[]{:S(2)}) collective-permute-start(bf16[20,1,180]{2,0,1:T(8,128)(2,1)S(1)} %get-tuple-element.15), channel_id=1, source_target_pairs={{0,8},{8,16},{16,24},{24,32},{32,40},{40,48},{48,56},{56,64},{64,7... | collective-permute-start | bytes 21608 | tf_op jit(solution)/shard_map/ppermute | solution.py:18
  46.4 5.9 %collective-permute-done.1 = bf16[20,1,180]{2,0,1:T(8,128)(2,1)S(1)} collective-permute-done((bf16[20,1,180]{2,0,1:T(8,128)(2,1)S(1)}, bf16[20,1,180]{2,0,1:T(8,128)(2,1)S(1)}, u32[]{:S(2)}, u32[]{:S(2)}) %collective-permute-start.1) | collective-permute-done | bytes 7232 | tf_op jit(solution)/shard_map/ppermute | solution.py:21
  53.2 3.0 %collective-permute-start.3 = (bf16[20,18,1]{2,0,1:T(8,128)(2,1)S(1)}, bf16[20,18,1]{2,0,1:T(8,128)(2,1)S(1)}, u32[]{:S(2)}, u32[]{:S(2)}) collective-permute-start(bf16[20,18,1]{2,0,1:T(8,128)(2,1)S(1)} %get-tuple-element.14), channel_id=1, source_target_pairs={{1,0},{2,1},{3,2},{4,3},{5,4},{6,5},{7,6},{0,7},{9,8},{10,9},{11,1... | collective-permute-start | bytes 2168 | tf_op jit(solution)/shard_map/ppermute | solution.py:21
  56.2 2.1 %collective-permute-done.2 = bf16[20,18,1]{2,0,1:T(8,128)(2,1)S(1)} collective-permute-done((bf16[20,18,1]{2,0,1:T(8,128)(2,1)S(1)}, bf16[20,18,1]{2,0,1:T(8,128)(2,1)S(1)}, u32[]{:S(2)}, u32[]{:S(2)}) %collective-permute-start.2) | collective-permute-done | bytes 752 | tf_op jit(solution)/shard_map/ppermute | solution.py:18
  61.1 1.0 fusion.45
  65.4 1.5 %maximum_convert_fusion.1 = bf16[16,180,256]{2,1,0:T(8,128)(2,1)S(1)} fusion(f32[16,180,256]{2,1,0:T(8,128)S(1)} %fusion.39, f32[16,180,256]{2,1,0:T(8,128)S(1)} %fusion.41, f32[16,180,256]{2,1,0:T(8,128)S(1)} %fusion.43, f32[16,180,256]{2,1,0:T(8,128)S(1)} %fusion.45, f32[16,180,256]{2,1,0:T(8,128)S(1)} %fusion.47, f32[16,180,256]{2,1,0:T(8,128)S(1)} %fusion.49, ...), kind=kOutput, calls=%fused_computation.1 | convolution fusion | flops 36864000 | bytes 25800704 | tf_op jit(solution)/shard_map/irc,io->rco/dot_general | solution.py:65
  66.9 1.6 %collective-permute-start.4 = (bf16[1,180,256]{2,1,0:T(8,128)(2,1)S(1)}, bf16[1,180,256]{2,1,0:T(8,128)(2,1)S(1)}, u32[]{:S(2)}, u32[]{:S(2)}) collective-permute-start(bf16[1,180,256]{2,1,0:T(8,128)(2,1)S(1)} %get-tuple-element.11), channel_id=1, source_target_pairs={{0,8},{8,16},{16,24},{24,32},{32,40},{40,48},{48,56},{56,64},{64,7... | collective-permute-start | bytes 276488 | tf_op jit(solution)/shard_map/ppermute | solution.py:18
  68.5 1.6 %collective-permute-done.4 = bf16[1,180,256]{2,1,0:T(8,128)(2,1)S(1)} collective-permute-done((bf16[1,180,256]{2,1,0:T(8,128)(2,1)S(1)}, bf16[1,180,256]{2,1,0:T(8,128)(2,1)S(1)}, u32[]{:S(2)}, u32[]{:S(2)}) %collective-permute-start.4) | collective-permute-done | bytes 92192 | tf_op jit(solution)/shard_map/ppermute | solution.py:18
  70.1 6.0 %collective-permute-done.5 = bf16[1,180,256]{2,1,0:T(8,128)(2,1)S(1)} collective-permute-done((bf16[1,180,256]{2,1,0:T(8,128)(2,1)S(1)}, bf16[1,180,256]{2,1,0:T(8,128)(2,1)S(1)}, u32[]{:S(2)}, u32[]{:S(2)}) %collective-permute-start.5) | collective-permute-done | bytes 92192 | tf_op jit(solution)/shard_map/ppermute | solution.py:21
  76.3 3.6 %collective-permute-start.7 = (bf16[18,1,256]{2,1,0:T(2,128)(2,1)S(1)}, bf16[18,1,256]{2,1,0:T(2,128)(2,1)S(1)}, u32[]{:S(2)}, u32[]{:S(2)}) collective-permute-start(bf16[18,1,256]{2,1,0:T(2,128)(2,1)S(1)} %get-tuple-element.8), channel_id=1, source_target_pairs={{1,0},{2,1},{3,2},{4,3},{5,4},{6,5},{7,6},{0,7},{9,8},{10,9},{11,1... | collective-permute-start | bytes 27656 | tf_op jit(solution)/shard_map/ppermute | solution.py:21
  79.8 1.1 collective-permute-done.6
  85.3 2.2 %fusion.31 = f32[16,180,256]{2,1,0:T(8,128)} fusion(bf16[18,182,256]{2,1,0:T(8,128)(2,1)S(1)} %maximum_select_fusion, bf16[3,3,256,256]{3,2,1,0:T(8,128)(2,1)S(1)} %copy-done), kind=kOutput, calls=%fused_computation.35 | convolution fusion | flops 377487360 | bytes 4587520 | tf_op jit(solution)/shard_map/rci,io->rco/dot_general | solution.py:78
  87.6 2.2 %fusion.33 = f32[16,180,256]{2,1,0:T(8,128)} fusion(bf16[18,182,256]{2,1,0:T(8,128)(2,1)S(1)} %maximum_select_fusion, bf16[3,3,256,256]{3,2,1,0:T(8,128)(2,1)S(1)} %copy-done), kind=kOutput, calls=%fused_computation.37 | convolution fusion | flops 377487360 | bytes 4587520 | tf_op jit(solution)/shard_map/rci,io->rco/dot_general | solution.py:78
  89.7 4.7 %maximum_convert_fusion = bf16[16,180,256]{2,1,0:T(8,128)(2,1)S(1)} fusion(f32[16,180,256]{2,1,0:T(8,128)S(1)} %fusion.19, f32[16,180,256]{2,1,0:T(8,128)S(1)} %fusion.21, f32[16,180,256]{2,1,0:T(8,128)S(1)} %fusion.23, f32[16,180,256]{2,1,0:T(8,128)S(1)} %fusion.25, f32[16,180,256]{2,1,0:T(8,128)S(1)} %fusion.27, f32[16,180,256]{2,1,0:T(8,128)S(1)} %fusion.29, ...), kind=kOutput, calls=%fused_computation | convolution fusion | flops 384860160 | bytes 27099136 | tf_op jit(solution)/shard_map/rci,io->rco/dot_general | solution.py:78
  94.5 1.2 %collective-permute-start.8 = (bf16[1,180,256]{2,1,0:T(8,128)(2,1)S(1)}, bf16[1,180,256]{2,1,0:T(8,128)(2,1)S(1)}, u32[]{:S(2)}, u32[]{:S(2)}) collective-permute-start(bf16[1,180,256]{2,1,0:T(8,128)(2,1)S(1)} %get-tuple-element.9), channel_id=1, source_target_pairs={{0,8},{8,16},{16,24},{24,32},{32,40},{40,48},{48,56},{56,64},{64,7... | collective-permute-start | bytes 276488 | tf_op jit(solution)/shard_map/ppermute | solution.py:18
  95.7 1.6 %collective-permute-done.8 = bf16[1,180,256]{2,1,0:T(8,128)(2,1)S(1)} collective-permute-done((bf16[1,180,256]{2,1,0:T(8,128)(2,1)S(1)}, bf16[1,180,256]{2,1,0:T(8,128)(2,1)S(1)}, u32[]{:S(2)}, u32[]{:S(2)}) %collective-permute-start.8) | collective-permute-done | bytes 92192 | tf_op jit(solution)/shard_map/ppermute | solution.py:18
  97.3 6.0 %collective-permute-done.9 = bf16[1,180,256]{2,1,0:T(8,128)(2,1)S(1)} collective-permute-done((bf16[1,180,256]{2,1,0:T(8,128)(2,1)S(1)}, bf16[1,180,256]{2,1,0:T(8,128)(2,1)S(1)}, u32[]{:S(2)}, u32[]{:S(2)}) %collective-permute-start.9) | collective-permute-done | bytes 92192 | tf_op jit(solution)/shard_map/ppermute | solution.py:21
  103.4 1.3 %collective-permute-start.10 = (bf16[18,1,256]{2,1,0:T(2,128)(2,1)S(1)}, bf16[18,1,256]{2,1,0:T(2,128)(2,1)S(1)}, u32[]{:S(2)}, u32[]{:S(2)}) collective-permute-start(bf16[18,1,256]{2,1,0:T(2,128)(2,1)S(1)} %get-tuple-element.5), channel_id=1, source_target_pairs={{0,1},{1,2},{2,3},{3,4},{4,5},{5,6},{6,7},{7,0},{8,9},{9,10},{10,1... | collective-permute-start | bytes 27656 | tf_op jit(solution)/shard_map/ppermute | solution.py:18
  104.6 2.6 %collective-permute-start.11 = (bf16[18,1,256]{2,1,0:T(2,128)(2,1)S(1)}, bf16[18,1,256]{2,1,0:T(2,128)(2,1)S(1)}, u32[]{:S(2)}, u32[]{:S(2)}) collective-permute-start(bf16[18,1,256]{2,1,0:T(2,128)(2,1)S(1)} %get-tuple-element.6), channel_id=1, source_target_pairs={{1,0},{2,1},{3,2},{4,3},{5,4},{6,5},{7,6},{0,7},{9,8},{10,9},{11,1... | collective-permute-start | bytes 27656 | tf_op jit(solution)/shard_map/ppermute | solution.py:21
  (57 shorter events, 21.1 us)
Async XLA Ops:
  34.6 23.9 %copy-start.1 = (bf16[3,3,20,256]{3,2,1,0:T(8,128)(2,1)S(1)}, bf16[3,3,20,256]{3,2,1,0:T(8,128)(2,1)}, u32[]{:S(2)}) copy-start(bf16[3,3,20,256]{3,2,1,0:T(8,128)(2,1)} %param.7) | copy-start | bytes 276484
  35.2 11.2 %collective-permute-start = (bf16[20,1,180]{2,0,1:T(8,128)(2,1)S(1)}, bf16[20,1,180]{2,0,1:T(8,128)(2,1)S(1)}, u32[]{:S(2)}, u32[]{:S(2)}) collective-permute-start(bf16[20,1,180]{2,0,1:T(8,128)(2,1)S(1)} %get-tuple-element.15), channel_id=1, source_target_pairs={{0,8},{8,16},{16,24},{24,32},{32,40},{40,48},{48,56},{56,64},{64,7... | collective-permute-start | bytes 21608 | tf_op jit(solution)/shard_map/ppermute | solution.py:18
  45.6 6.7 %collective-permute-start.1 = (bf16[20,1,180]{2,0,1:T(8,128)(2,1)S(1)}, bf16[20,1,180]{2,0,1:T(8,128)(2,1)S(1)}, u32[]{:S(2)}, u32[]{:S(2)}) collective-permute-start(bf16[20,1,180]{2,0,1:T(8,128)(2,1)S(1)} %get-tuple-element.16), channel_id=1, source_target_pairs={{8,0},{16,8},{24,16},{32,24},{40,32},{48,40},{56,48},{64,56},{72,6... | collective-permute-start | bytes 21608 | tf_op jit(solution)/shard_map/ppermute | solution.py:21
  52.5 5.8 %collective-permute-start.2 = (bf16[20,18,1]{2,0,1:T(8,128)(2,1)S(1)}, bf16[20,18,1]{2,0,1:T(8,128)(2,1)S(1)}, u32[]{:S(2)}, u32[]{:S(2)}) collective-permute-start(bf16[20,18,1]{2,0,1:T(8,128)(2,1)S(1)} %get-tuple-element.13), channel_id=1, source_target_pairs={{0,1},{1,2},{2,3},{3,4},{4,5},{5,6},{6,7},{7,0},{8,9},{9,10},{10,1... | collective-permute-start | bytes 2168 | tf_op jit(solution)/shard_map/ppermute | solution.py:18
  53.2 5.1 %collective-permute-start.3 = (bf16[20,18,1]{2,0,1:T(8,128)(2,1)S(1)}, bf16[20,18,1]{2,0,1:T(8,128)(2,1)S(1)}, u32[]{:S(2)}, u32[]{:S(2)}) collective-permute-start(bf16[20,18,1]{2,0,1:T(8,128)(2,1)S(1)} %get-tuple-element.14), channel_id=1, source_target_pairs={{1,0},{2,1},{3,2},{4,3},{5,4},{6,5},{7,6},{0,7},{9,8},{10,9},{11,1... | collective-permute-start | bytes 2168 | tf_op jit(solution)/shard_map/ppermute | solution.py:21
  66.9 3.2 %collective-permute-start.4 = (bf16[1,180,256]{2,1,0:T(8,128)(2,1)S(1)}, bf16[1,180,256]{2,1,0:T(8,128)(2,1)S(1)}, u32[]{:S(2)}, u32[]{:S(2)}) collective-permute-start(bf16[1,180,256]{2,1,0:T(8,128)(2,1)S(1)} %get-tuple-element.11), channel_id=1, source_target_pairs={{0,8},{8,16},{16,24},{24,32},{32,40},{40,48},{48,56},{56,64},{64,7... | collective-permute-start | bytes 276488 | tf_op jit(solution)/shard_map/ppermute | solution.py:18
  68.5 7.6 %collective-permute-start.5 = (bf16[1,180,256]{2,1,0:T(8,128)(2,1)S(1)}, bf16[1,180,256]{2,1,0:T(8,128)(2,1)S(1)}, u32[]{:S(2)}, u32[]{:S(2)}) collective-permute-start(bf16[1,180,256]{2,1,0:T(8,128)(2,1)S(1)} %get-tuple-element.12), channel_id=1, source_target_pairs={{8,0},{16,8},{24,16},{32,24},{40,32},{48,40},{56,48},{64,56},{72,6... | collective-permute-start | bytes 276488 | tf_op jit(solution)/shard_map/ppermute | solution.py:21
  76.2 4.8 %collective-permute-start.6 = (bf16[18,1,256]{2,1,0:T(2,128)(2,1)S(1)}, bf16[18,1,256]{2,1,0:T(2,128)(2,1)S(1)}, u32[]{:S(2)}, u32[]{:S(2)}) collective-permute-start(bf16[18,1,256]{2,1,0:T(2,128)(2,1)S(1)} %get-tuple-element.7), channel_id=1, source_target_pairs={{0,1},{1,2},{2,3},{3,4},{4,5},{5,6},{6,7},{7,0},{8,9},{9,10},{10,1... | collective-permute-start | bytes 27656 | tf_op jit(solution)/shard_map/ppermute | solution.py:18
  76.2 5.7 %copy-start = (bf16[3,3,256,256]{3,2,1,0:T(8,128)(2,1)S(1)}, bf16[3,3,256,256]{3,2,1,0:T(8,128)(2,1)}, u32[]{:S(2)}) copy-start(bf16[3,3,256,256]{3,2,1,0:T(8,128)(2,1)} %param.8) | copy-start | bytes 3538948
  76.3 4.7 %collective-permute-start.7 = (bf16[18,1,256]{2,1,0:T(2,128)(2,1)S(1)}, bf16[18,1,256]{2,1,0:T(2,128)(2,1)S(1)}, u32[]{:S(2)}, u32[]{:S(2)}) collective-permute-start(bf16[18,1,256]{2,1,0:T(2,128)(2,1)S(1)} %get-tuple-element.8), channel_id=1, source_target_pairs={{1,0},{2,1},{3,2},{4,3},{5,4},{6,5},{7,6},{0,7},{9,8},{10,9},{11,1... | collective-permute-start | bytes 27656 | tf_op jit(solution)/shard_map/ppermute | solution.py:21
  94.5 2.8 %collective-permute-start.8 = (bf16[1,180,256]{2,1,0:T(8,128)(2,1)S(1)}, bf16[1,180,256]{2,1,0:T(8,128)(2,1)S(1)}, u32[]{:S(2)}, u32[]{:S(2)}) collective-permute-start(bf16[1,180,256]{2,1,0:T(8,128)(2,1)S(1)} %get-tuple-element.9), channel_id=1, source_target_pairs={{0,8},{8,16},{16,24},{24,32},{32,40},{40,48},{48,56},{56,64},{64,7... | collective-permute-start | bytes 276488 | tf_op jit(solution)/shard_map/ppermute | solution.py:18
  95.7 7.6 %collective-permute-start.9 = (bf16[1,180,256]{2,1,0:T(8,128)(2,1)S(1)}, bf16[1,180,256]{2,1,0:T(8,128)(2,1)S(1)}, u32[]{:S(2)}, u32[]{:S(2)}) collective-permute-start(bf16[1,180,256]{2,1,0:T(8,128)(2,1)S(1)} %get-tuple-element.10), channel_id=1, source_target_pairs={{8,0},{16,8},{24,16},{32,24},{40,32},{48,40},{56,48},{64,56},{72,6... | collective-permute-start | bytes 276488 | tf_op jit(solution)/shard_map/ppermute | solution.py:21
  103.4 4.8 %collective-permute-start.10 = (bf16[18,1,256]{2,1,0:T(2,128)(2,1)S(1)}, bf16[18,1,256]{2,1,0:T(2,128)(2,1)S(1)}, u32[]{:S(2)}, u32[]{:S(2)}) collective-permute-start(bf16[18,1,256]{2,1,0:T(2,128)(2,1)S(1)} %get-tuple-element.5), channel_id=1, source_target_pairs={{0,1},{1,2},{2,3},{3,4},{4,5},{5,6},{6,7},{7,0},{8,9},{9,10},{10,1... | collective-permute-start | bytes 27656 | tf_op jit(solution)/shard_map/ppermute | solution.py:18
  104.6 4.5 %copy-start.2 = (bf16[3,3,256,1]{2,1,3,0:T(4,128)(2,1)S(1)}, bf16[3,3,256,1]{2,1,3,0:T(4,128)(2,1)}, u32[]{:S(2)}) copy-start(bf16[3,3,256,1]{2,1,3,0:T(4,128)(2,1)} %param.9) | copy-start | bytes 13828
  104.6 3.5 %collective-permute-start.11 = (bf16[18,1,256]{2,1,0:T(2,128)(2,1)S(1)}, bf16[18,1,256]{2,1,0:T(2,128)(2,1)S(1)}, u32[]{:S(2)}, u32[]{:S(2)}) collective-permute-start(bf16[18,1,256]{2,1,0:T(2,128)(2,1)S(1)} %get-tuple-element.6), channel_id=1, source_target_pairs={{1,0},{2,1},{3,2},{4,3},{5,4},{6,5},{7,6},{0,7},{9,8},{10,9},{11,1... | collective-permute-start | bytes 27656 | tf_op jit(solution)/shard_map/ppermute | solution.py:21
where the time goes:
time: 116 us; the launch traced here: 114 us
  matrix products  30.4 us (26%)
  waiting for transfers between devices  26.1 us (22%)
  starting transfers between devices  24.3 us (21%)
  blocking collectives  23.7 us (20%)
  local copies, waits for them, and re-layouts  6.69 us (6%)
  other arithmetic  3 us (3%)
    all_gather x1, blocking collectives, per_device(): lax.all_gather(kept_modes, 'lon', axis=3, tiled=True)  23.7 us
    ppermute x6, waiting for transfers between devices, padded_2(): lax.ppermute(lax.slice_in_dim(block, 0, width, axis=dim), axis, backward)  17.9 us
    ppermute x6, starting transfers between devices, padded_2(): lax.ppermute(lax.slice_in_dim(block, block.shape[dim] - width, None, axis...  15.2 us
    dot_general x9, matrix products, conv_valid(): jnp.einsum('rci,io->rco', window, weight[row_off, col_off], preferred_ele...  12.5 us
    ppermute x6, starting transfers between devices, padded_2(): lax.ppermute(lax.slice_in_dim(block, 0, width, axis=dim), axis, backward)  9.19 us
    dot_general x9, matrix products, conv_channels_first(): jnp.einsum('irc,io->rco', window, weight[row_off, col_off], preferred_ele...  8.43 us
    ppermute x6, waiting for transfers between devices, padded_2(): lax.ppermute(lax.slice_in_dim(block, block.shape[dim] - width, None, axis...  8.18 us
    dot_general x9, matrix products, conv_single(): jnp.einsum('rci,i->rc', window, weight[row_off, col_off, :, 0], preferred...  4.63 us
  transfers between devices with their start and end apart: 12, of which 9 were waited for; matrix products, arithmetic and copies ran while one was open for 0% of the time, Pallas kernels for 0%

commit v1 on v0

v1 whole, which is shorter than its diff:
```python
import math

import jax
import jax.numpy as jnp
import numpy as np
from jax import lax
from jax.experimental import pallas as pl
from jax.experimental.pallas import tpu as pltpu
from jax.sharding import PartitionSpec as P

MESH = pl.DeviceIdType.MESH
BF16 = jnp.bfloat16
F32 = jnp.float32

LON_TOK = 180
PATCH = 8
NLON = 8
COLS = 180
ROWS = 16
OUT = 20
CH = 256
TQ = 3
CG = 8
TOK = TQ * CG
RG = 2
RJ = 9
T = TQ * PATCH
SUB = RG * CG
FIRST_J = RJ + 2
PIX_J = RJ + 4
WIN = (T + 2) // 2
PITCH = (T + 2) * SUB
ROWL = PATCH * OUT


def first_token(sector):
    return (COLS * sector - 3) // PATCH


def dft_table(mode_count):
    ids = []
    for d in range(NLON):
        for tq in range(TQ):
            for cg in range(CG):
                ids.append((first_token(d) + cg * TQ + tq) % LON_TOK)
    modes = np.arange(mode_count)
    angle = (np.array(ids)[:, None] * modes[None, :] % LON_TOK) * (2.0 * math.pi / LON_TOK)
    scale = np.where(modes == 0, 1.0, 2.0) / math.sqrt(LON_TOK)
    table = np.stack([scale * np.cos(angle), -scale * np.sin(angle)], axis=2)
    table = table.reshape(len(ids), 2 * mode_count).astype(np.float32)
    high = table.astype(BF16)
    low = (table - high.astype(np.float32)).astype(BF16)
    return np.concatenate([high, low], axis=0)


def order_table():
    table = np.zeros((2, 3 * T * SUB, RG * CH), np.float32)
    for parity in range(2):
        offset = COLS * parity - PATCH * first_token(parity)
        for b in range(3):
            for q in range(COLS):
                col = q + offset - 1 + b
                cg, t = divmod(col, T)
                for rg in range(RG):
                    table[parity, b * T * SUB + t * SUB + rg * CG + cg, rg * CH + q] = 1.0
    return table.astype(BF16)


def exchange_kernel(
    modes_ref, table_ref, order_ref, dec_ref, in_ref, mid_ref, out_ref,
    field, dec_v, in_v, mid_v, out_v, order_v,
    modes_s, table_s, send, in_s, out_s, out_f,
    local_sem, dec_sem, send_sem, recv_sem,
):
    lat, lon = lax.axis_index("lat"), lax.axis_index("lon")
    nlat = lax.axis_size("lat")
    up, down = lax.rem(lat + nlat - 1, nlat), lax.rem(lat + 1, nlat)
    chans = modes_s.shape[3]
    mode_count = modes_s.shape[1]

    early = [
        pltpu.make_async_copy(modes_ref, modes_s, local_sem.at[0]),
        pltpu.make_async_copy(table_ref, table_s, local_sem.at[1]),
    ]
    late = [
        pltpu.make_async_copy(in_ref, in_s, local_sem.at[2]),
        pltpu.make_async_copy(out_ref, out_s, local_sem.at[3]),
    ]
    last = [
        pltpu.make_async_copy(
            dec_ref.at[k * chans : (k + 1) * chans], dec_v.at[k, 0:chans], dec_sem.at[k]
        )
        for k in range(NLON)
    ] + [
        pltpu.make_async_copy(mid_ref, mid_v, local_sem.at[4]),
        pltpu.make_async_copy(order_ref.at[lax.rem(lon, 2)], order_v, local_sem.at[5]),
    ]
    for copy in early:
        copy.start()
    barrier = pltpu.get_barrier_semaphore()
    for step in range(NLON):
        there = lax.rem(lon + step, NLON)
        for row in (up, down) if step == 0 else (up, down, lat):
            pl.semaphore_signal(
                barrier, inc=1, device_id={"lat": row, "lon": there}, device_id_type=MESH
            )
    for copy in late + last:
        copy.start()
    send[...] = jnp.zeros_like(send)
    for copy in early:
        copy.wait()
    for row in range(2):
        values = modes_s[row].reshape(2 * mode_count, chans)
        wide = jnp.dot(table_s[...], values, preferred_element_type=F32)
        half = wide.shape[0] // 2
        whole = (wide[:half] + wide[half:]).astype(BF16)
        send[:, row, :, 0:chans] = whole.reshape(NLON, TOK, chans)
    field[lon, 1:3] = send[lon]
    pl.semaphore_wait(barrier, 3 * NLON - 1)
    sends, receives = [], []
    for step in range(NLON):
        there = lax.rem(lon + step, NLON)
        origin = lax.rem(lon + NLON - step, NLON)
        for way, (row, source, target) in enumerate(
            ((up, 0, 3), (down, 1, 0), (lat, None, None))
        ):
            if way == 2 and step == 0:
                continue
            copy = pltpu.make_async_remote_copy(
                src_ref=send.at[there] if way == 2 else send.at[there, source],
                dst_ref=field.at[lon, 1:3] if way == 2 else field.at[lon, target],
                send_sem=send_sem.at[way, step],
                recv_sem=recv_sem.at[way, step],
                device_id={"lat": row, "lon": there},
                device_id_type=MESH,
            )
            copy.start()
            sends.append(copy)
            receives.append(
                pltpu.make_async_remote_copy(
                    src_ref=send.at[there] if way == 2 else send.at[there, source],
                    dst_ref=field.at[origin, 1:3] if way == 2 else field.at[origin, target],
                    send_sem=send_sem.at[way, step],
                    recv_sem=recv_sem.at[way, step],
                    device_id={"lat": row, "lon": there},
                    device_id_type=MESH,
                )
            )
    for copy in late:
        copy.wait()
    dec_v[:, chans:, :] = jnp.zeros((NLON, dec_v.shape[1] - chans, dec_v.shape[2]), BF16)
    for turn in range(3):
        for phase in range(2):
            rows = []
            for place in range(3):
                a = (place - turn) % 3
                if phase:
                    rows.append(jnp.zeros((OUT, CH), BF16))
                rows += [in_s[a, b] for b in range(3)]
                if not phase:
                    rows.append(jnp.zeros((OUT, CH), BF16))
            rows.append(jnp.zeros((16, CH), BF16))
            in_v[turn, :, phase * CH : (phase + 1) * CH] = jnp.concatenate(rows, axis=0)
    out_f[...] = jnp.zeros_like(out_f)
    for a in range(3):
        for b in range(3):
            out_f[b * 8 + a : b * 8 + a + 1, :] = out_s[a, b : b + 1, :].astype(F32)
    out_v[...] = out_f[...].astype(BF16)
    for copy in last:
        copy.wait()
    for copy in receives:
        copy.wait_recv()
    for copy in sends:
        copy.wait_send()


def head_kernel(
    field, dec_v, in_v, mid_v, out_v, order_v, result, tokens, pieces, first, taps, sums
):
    lat = lax.axis_index("lat")
    top, bottom = lat == 0, lat == lax.axis_size("lat") - 1
    flat = jnp.concatenate([field[k].reshape(4 * TOK, 128) for k in range(NLON)], axis=1)
    decoded = jnp.dot(
        flat, dec_v[...].reshape(NLON * 128, ROWL * PATCH), preferred_element_type=F32
    ).reshape(4, TQ, CG, ROWL * PATCH)
    tokens[0] = jnp.where(top, 0.0, decoded[0])
    tokens[1:3] = decoded[1:3]
    tokens[3] = jnp.where(bottom, 0.0, decoded[3])

    lane = lax.broadcasted_iota(jnp.int32, (CG, CH), 1)

    def placed(slot, tq, start, place):
        base = min(start // 128 * 128, ROWL * PATCH - CH)
        block = tokens[slot, tq, :, base : base + CH]
        shift = (place - (start - base)) % CH
        return pltpu.roll(block, shift, 1) if shift else block

    halves = {}
    for p in range(-3, 19):
        slot, pr, place = p // PATCH + 1, p % PATCH, p % 3 * 80
        for w in range(WIN - 1):
            tq, part = divmod(w, 4)
            if part:
                value = placed(slot, tq, pr * ROWL + (part - 1) * 40, place)
            else:
                before = placed(slot, (tq - 1) % TQ, pr * ROWL + 120, place)
                if tq == 0:
                    before = pltpu.roll(before, 1, 0)
                own = placed(slot, tq, pr * ROWL, place + 40)
                value = jnp.where(lane < place + 40, before, own)
            halves[p, w] = value
        before = placed(slot, TQ - 1, pr * ROWL + 120, place)
        after = pltpu.roll(placed(slot, 0, pr * ROWL, place + 40), CG - 1, 0)
        halves[p, WIN - 1] = jnp.where(lane < place + 40, before, after)
        if p >= 6:
            for w in range(WIN):
                pieces[p - 6, w] = jnp.concatenate(
                    [halves.pop((p - 9, w)), halves[p, w]], axis=0
                ).astype(BF16)

    lane2 = lax.broadcasted_iota(jnp.int32, (SUB, CH), 1)
    side = lax.broadcasted_iota(jnp.int32, (SUB, CH), 0) // CG
    for j in range(FIRST_J):
        ordered = [pieces[j + (c - j) % 3] for c in range(3)]
        window = jnp.where(
            lane2 < 80, ordered[0], jnp.where(lane2 < 160, ordered[1], ordered[2])
        ).reshape(WIN * SUB, CH)
        hidden = jnp.maximum(
            jnp.dot(window, in_v[j % 3], preferred_element_type=F32), 0.0
        ).reshape(WIN, SUB, 2 * CH)
        for phase in range(2):
            part = hidden[:, :, phase * CH : (phase + 1) * CH]
            if j < 2:
                part = jnp.where((side == 0) & top, 0.0, part)
            if j >= RJ:
                part = jnp.where((side == 1) & bottom, 0.0, part)
            first[j, :, phase * SUB : (phase + 1) * SUB, :] = part.astype(BF16)

    def mid_row(j, carry):
        blocks = []
        for a in range(3):
            for b in range(3):
                rows = first[j + a].reshape(PITCH, CH)
                blocks.append(rows[b * SUB : b * SUB + T * SUB])
        second = jnp.dot(
            jnp.concatenate(blocks, axis=1), mid_v[...], preferred_element_type=F32
        )
        second = jnp.maximum(second, 0.0).reshape(T, SUB, CH)
        outside = ((side == 0) & top & (j == 0)) | ((side == 1) & bottom & (j == RJ - 1))
        second = jnp.where(outside, 0.0, second).astype(BF16).reshape(T * SUB, CH)
        tap = lax.dot_general(
            out_v[...], second, (((1,), (1,)), ((), ())), preferred_element_type=F32
        )
        taps[j] = jnp.concatenate([tap[b * 8 : b * 8 + 8] for b in range(3)], axis=1)
        return carry

    lax.fori_loop(0, RJ, mid_row, 0)
    tap = taps[...].reshape(RJ * 8, 3 * T * SUB)
    high = tap.astype(BF16)
    low = (tap - high.astype(F32)).astype(BF16)
    moved = jnp.dot(
        jnp.concatenate([high, low], axis=0), order_v[...], preferred_element_type=F32
    )
    sums[...] = moved[: RJ * 8] + moved[RJ * 8 :]
    for p in range(ROWS):
        total = None
        for a in range(3):
            rg, j = divmod(p + a, RJ)
            term = sums[j * 8 + a : j * 8 + a + 1, rg * CH : rg * CH + COLS]
            total = term if total is None else total + term
        result[p : p + 1, :] = total


def per_device(kept_modes, decoder_weight, conv_in_weight, conv_mid_weight, conv_out_weight):
    mode_count, chans = kept_modes.shape[1], kept_modes.shape[3]
    table = dft_table(mode_count)
    order = order_table()
    vmem = pl.BlockSpec(memory_space=pltpu.VMEM)
    anywhere = pl.BlockSpec(memory_space=pl.ANY)
    dma = pltpu.SemaphoreType.DMA
    staged = pl.pallas_call(
        exchange_kernel,
        out_shape=(
            pltpu.VMEM((NLON, 4, TOK, 128), BF16),
            pltpu.VMEM((NLON, 128, ROWL * PATCH), BF16),
            pltpu.VMEM((3, CH, 2 * CH), BF16),
            pltpu.VMEM((9 * CH, CH), BF16),
            pltpu.VMEM((24, CH), BF16),
            pltpu.VMEM(order.shape[1:], BF16),
        ),
        in_specs=[anywhere] * 7,
        out_specs=(vmem,) * 6,
        scratch_shapes=[
            pltpu.VMEM(kept_modes.shape, BF16),
            pltpu.VMEM(table.shape, BF16),
            pltpu.VMEM((NLON, 2, TOK, 128), BF16),
            pltpu.VMEM(conv_in_weight.shape, BF16),
            pltpu.VMEM((3, 3, CH), BF16),
            pltpu.VMEM((24, CH), F32),
            dma((6,)),
            dma((NLON,)),
            dma((3, NLON)),
            dma((3, NLON)),
        ],
        compiler_params=pltpu.CompilerParams(
            collective_id=0, has_side_effects=True, vmem_limit_bytes=24 * 2**20
        ),
        name="exchange",
    )(
        kept_modes,
        jnp.asarray(table),
        jnp.asarray(order),
        decoder_weight,
        conv_in_weight,
        conv_mid_weight.reshape(9 * CH, CH),
        conv_out_weight.reshape(3, 3, CH),
    )
    staged = [pltpu.with_memory_space_constraint(x, pltpu.VMEM) for x in staged]
    return pl.pallas_call(
        head_kernel,
        out_shape=jax.ShapeDtypeStruct((ROWS, COLS), F32),
        in_specs=[vmem] * 6,
        out_specs=vmem,
        scratch_shapes=[
            pltpu.VMEM((4, TQ, CG, ROWL * PATCH), F32),
            pltpu.VMEM((PIX_J, WIN, SUB, CH), BF16),
            pltpu.VMEM((FIRST_J, WIN, 2 * SUB, CH), BF16),
            pltpu.VMEM((RJ, 8, 3 * T * SUB), F32),
            pltpu.VMEM((RJ * 8, RG * CH), F32),
        ],
        compiler_params=pltpu.CompilerParams(vmem_limit_bytes=32 * 2**20),
        name="head",
    )(*staged)


def solution(mesh):
    placed = (P("lat", None, None, "lon"), P(), P(), P(), P())
    return jax.shard_map(
        per_device, mesh=mesh, in_specs=placed, out_specs=P("lat", "lon"), check_vma=False
    )
```

time: 116 us -> 33.8 us (0.29)
  the two profiles are of different devices: /device:TPU:103 before, /device:TPU:1 now
where the time goes in v1:
time: 33.8 us; the launch traced here: 33.5 us
  Pallas kernels  25.6 us (76%)
  local copies, waits for them, and re-layouts  7.88 us (23%)
    pallas_call x1, Pallas kernels, per_device(): pl.pallas_call(exchange_kernel, out_shape=(pltpu.VMEM((NLON, 4, TOK, 128)...  15.9 us
    pallas_call x1, Pallas kernels, per_device(): pl.pallas_call(head_kernel, out_shape=jax.ShapeDtypeStruct((ROWS, COLS),...  9.7 us
    unnamed x14, local copies, waits for them, and re-layouts  7.88 us

profile of v1, /device:TPU:1, one launch (start us, length us, event | category | flops | bytes accessed | tf_op | source)
XLA Modules:
  0.0 33.5 jit_solution(4534172994806992344)
XLA Ops:
  0.0 0.0 copy-start
  0.0 1.7 %copy-done = bf16[2,1152,512]{2,1,0:T(8,128)(2,1)S(1)} copy-done((bf16[2,1152,512]{2,1,0:T(8,128)(2,1)S(1)}, bf16[2,1152,512]{2,1,0:T(8,128)(2,1)}, u32[]{:S(2)}) %copy-start) | copy-done | bytes 2359320
  1.7 0.0 copy-start.1
  1.7 1.5 %copy-done.1 = bf16[768,1280]{1,0:T(8,128)(2,1)S(1)} copy-done((bf16[768,1280]{1,0:T(8,128)(2,1)S(1)}, bf16[768,1280]{1,0:T(8,128)(2,1)}, u32[]{:S(2)}) %copy-start.1) | copy-done | bytes 1966104
  3.2 0.0 copy-start.2
  3.2 1.3 %copy-done.2 = bf16[3,3,256,256]{3,2,1,0:T(8,128)(2,1)S(1)} copy-done((bf16[3,3,256,256]{3,2,1,0:T(8,128)(2,1)S(1)}, bf16[3,3,256,256]{3,2,1,0:T(8,128)(2,1)}, u32[]{:S(2)}) %copy-start.2) | copy-done | bytes 1179672
  4.5 0.0 copy-start.3
  4.5 0.9 %copy-done.3 = bf16[384,180]{1,0:T(8,128)(2,1)S(1)} copy-done((bf16[384,180]{1,0:T(8,128)(2,1)S(1)}, bf16[384,180]{1,0:T(8,128)(2,1)}, u32[]{:S(2)}) %copy-start.3) | copy-done | bytes 138264
  5.4 0.0 copy-start.4
  5.4 0.9 %copy-done.4 = bf16[3,3,20,256]{3,2,1,0:T(8,128)(2,1)S(1)} copy-done((bf16[3,3,20,256]{3,2,1,0:T(8,128)(2,1)S(1)}, bf16[3,3,20,256]{3,2,1,0:T(8,128)(2,1)}, u32[]{:S(2)}) %copy-start.4) | copy-done | bytes 92184
  6.3 0.0 copy-start.5
  6.3 0.9 %copy-done.5 = bf16[2,90,2,96]{3,2,1,0:T(2,128)(2,1)S(1)} copy-done((bf16[2,90,2,96]{3,2,1,0:T(2,128)(2,1)S(1)}, bf16[2,90,2,96]{3,2,1,0:T(2,128)(2,1)}, u32[]{:S(2)}) %copy-start.5) | copy-done | bytes 69144
  7.2 0.0 copy-start.6
  7.2 0.7 %copy-done.6 = bf16[3,3,256,1]{2,1,3,0:T(4,128)(2,1)S(1)} copy-done((bf16[3,3,256,1]{2,1,3,0:T(4,128)(2,1)S(1)}, bf16[3,3,256,1]{2,1,3,0:T(4,128)(2,1)}, u32[]{:S(2)}) %copy-start.6) | copy-done | bytes 4632
  7.9 15.9 %exchange.1 = (bf16[8,4,24,128]{3,2,1,0:T(8,128)(2,1)S(1)}, bf16[8,128,1280]{2,1,0:T(8,128)(2,1)S(1)}, bf16[3,256,512]{2,1,0:T(8,128)(2,1)S(1)}, bf16[2304,256]{...) custom-call(bf16[2,90,2,96]{3,2,1,0:T(2,128)(2,1)S(1)} %copy-done.5, ...), custom_call_target="tpu_custom_call" | custom-call | tf_op jit(solution)/shard_map/exchange/pallas_call | solution.py:281
  23.8 9.7 %head.1 = f32[16,180]{1,0:T(8,128)} custom-call(bf16[8,4,24,128]{3,2,1,0:T(8,128)(2,1)S(1)} %get-tuple-element.11.field, bf16[8,128,1280]{2,1,0:T(8,128)(2,1)S(1)} %get-tuple-element.12.dec_v, bf16[3,256,512]{2,1,0:T(8,128)(2,1)S(1)} %get-tuple-element.13.in_v, bf16[2304,256]{1,0:T(8,128)(2,1)S(1)} %get-tuple-element.14.mid_v, ...), custom_call_target="tpu_custom_call" | custom-call | tf_op jit(solution)/shard_map/head/pallas_call | solution.py:319
Async XLA Ops:
  0.0 1.7 %copy-start = (bf16[2,1152,512]{2,1,0:T(8,128)(2,1)S(1)}, bf16[2,1152,512]{2,1,0:T(8,128)(2,1)}, u32[]{:S(2)}) copy-start(bf16[2,1152,512]{2,1,0:T(8,128)(2,1)} %constant.5.clone.order_ref) | copy-start | bytes 7077892
  1.7 1.5 %copy-start.1 = (bf16[768,1280]{1,0:T(8,128)(2,1)S(1)}, bf16[768,1280]{1,0:T(8,128)(2,1)}, u32[]{:S(2)}) copy-start(bf16[768,1280]{1,0:T(8,128)(2,1)} %dec_ref.1) | copy-start | bytes 5898244
  3.2 1.3 %copy-start.2 = (bf16[3,3,256,256]{3,2,1,0:T(8,128)(2,1)S(1)}, bf16[3,3,256,256]{3,2,1,0:T(8,128)(2,1)}, u32[]{:S(2)}) copy-start(bf16[3,3,256,256]{3,2,1,0:T(8,128)(2,1)} %param.10) | copy-start | bytes 3538948
  4.5 0.9 %copy-start.3 = (bf16[384,180]{1,0:T(8,128)(2,1)S(1)}, bf16[384,180]{1,0:T(8,128)(2,1)}, u32[]{:S(2)}) copy-start(bf16[384,180]{1,0:T(8,128)(2,1)} %constant.4.clone.table_ref) | copy-start | bytes 414724
  5.4 0.9 %copy-start.4 = (bf16[3,3,20,256]{3,2,1,0:T(8,128)(2,1)S(1)}, bf16[3,3,20,256]{3,2,1,0:T(8,128)(2,1)}, u32[]{:S(2)}) copy-start(bf16[3,3,20,256]{3,2,1,0:T(8,128)(2,1)} %in_ref.1) | copy-start | bytes 276484
  6.3 0.9 %copy-start.5 = (bf16[2,90,2,96]{3,2,1,0:T(2,128)(2,1)S(1)}, bf16[2,90,2,96]{3,2,1,0:T(2,128)(2,1)}, u32[]{:S(2)}) copy-start(bf16[2,90,2,96]{3,2,1,0:T(2,128)(2,1)} %modes_ref.1) | copy-start | bytes 207364
  7.2 0.7 %copy-start.6 = (bf16[3,3,256,1]{2,1,3,0:T(4,128)(2,1)S(1)}, bf16[3,3,256,1]{2,1,3,0:T(4,128)(2,1)}, u32[]{:S(2)}) copy-start(bf16[3,3,256,1]{2,1,3,0:T(4,128)(2,1)} %param.11) | copy-start | bytes 13828

commit v2 on v1

--- a/solution.py
+++ b/solution.py
@@ -276,7 +276,7 @@
     table = dft_table(mode_count)
     order = order_table()
     vmem = pl.BlockSpec(memory_space=pltpu.VMEM)
-    anywhere = pl.BlockSpec(memory_space=pl.ANY)
+    anywhere = pl.BlockSpec(memory_space=pltpu.HBM)
     dma = pltpu.SemaphoreType.DMA
     staged = pl.pallas_call(
         exchange_kernel,
@@ -307,13 +307,18 @@
         ),
         name="exchange",
     )(
-        kept_modes,
-        jnp.asarray(table),
-        jnp.asarray(order),
-        decoder_weight,
-        conv_in_weight,
-        conv_mid_weight.reshape(9 * CH, CH),
-        conv_out_weight.reshape(3, 3, CH),
+        *[
+            pltpu.with_memory_space_constraint(x, pltpu.HBM)
+            for x in (
+                kept_modes,
+                jnp.asarray(table),
+                jnp.asarray(order),
+                decoder_weight,
+                conv_in_weight,
+                conv_mid_weight.reshape(9 * CH, CH),
+                conv_out_weight.reshape(3, 3, CH),
+            )
+        ]
     )
     staged = [pltpu.with_memory_space_constraint(x, pltpu.VMEM) for x in staged]
     return pl.pallas_call(

time: 33.8 us -> 25.7 us (0.76)
  local copies, waits for them, and re-layouts: 7.88 us -> 0 us
    unnamed x14 -> x0, local copies, waits for them, and re-layouts: 7.88 us -> none
where the time goes in v2:
time: 25.7 us; the launch traced here: 25.6 us
  Pallas kernels  25.6 us (100%)
    pallas_call x1, Pallas kernels, per_device(): pl.pallas_call(exchange_kernel, out_shape=(pltpu.VMEM((NLON, 4, TOK, 128)...  15.9 us
    pallas_call x1, Pallas kernels, per_device(): pl.pallas_call(head_kernel, out_shape=jax.ShapeDtypeStruct((ROWS, COLS),...  9.7 us

profile of v2, /device:TPU:1, one launch (start us, length us, event | category | flops | bytes accessed | tf_op | source)
XLA Modules:
  0.0 25.6 jit_solution(6709275307790584085)
XLA Ops:
  0.0 15.9 %exchange.1 = (bf16[8,4,24,128]{3,2,1,0:T(8,128)(2,1)S(1)}, bf16[8,128,1280]{2,1,0:T(8,128)(2,1)S(1)}, bf16[3,256,512]{2,1,0:T(8,128)(2,1)S(1)}, bf16[2304,256]{...) custom-call(bf16[2,90,2,96]{3,2,1,0:T(2,128)(2,1)} %modes_ref.1, ...), custom_call_target="tpu_custom_call" | custom-call | tf_op jit(solution)/shard_map/exchange/pallas_call | solution.py:281
  15.9 9.7 %head.1 = f32[16,180]{1,0:T(8,128)} custom-call(bf16[8,4,24,128]{3,2,1,0:T(8,128)(2,1)S(1)} %get-tuple-element.11.field, bf16[8,128,1280]{2,1,0:T(8,128)(2,1)S(1)} %get-tuple-element.12.dec_v, bf16[3,256,512]{2,1,0:T(8,128)(2,1)S(1)} %get-tuple-element.13.in_v, bf16[2304,256]{1,0:T(8,128)(2,1)S(1)} %get-tuple-element.14.mid_v, ...), custom_call_target="tpu_custom_call" | custom-call | tf_op jit(solution)/shard_map/head/pallas_call | solution.py:324

commit v3 on v2

--- a/solution.py
+++ b/solution.py
@@ -28,8 +28,10 @@
 SUB = RG * CG
 FIRST_J = RJ + 2
 PIX_J = RJ + 4
+JB = 3
 WIN = (T + 2) // 2
-PITCH = (T + 2) * SUB
+PAIRS = T // 2
+STEP = PAIRS * SUB
 ROWL = PATCH * OUT
 
 
@@ -61,20 +63,21 @@
             for q in range(COLS):
                 col = q + offset - 1 + b
                 cg, t = divmod(col, T)
+                pair, phase = divmod(t, 2)
+                at = (b * 2 + phase) * STEP + pair * SUB + cg
                 for rg in range(RG):
-                    table[parity, b * T * SUB + t * SUB + rg * CG + cg, rg * CH + q] = 1.0
+                    table[parity, at + rg * CG, rg * CH + q] = 1.0
     return table.astype(BF16)
 
 
 def exchange_kernel(
     modes_ref, table_ref, order_ref, dec_ref, in_ref, mid_ref, out_ref,
     field, dec_v, in_v, mid_v, out_v, order_v,
-    modes_s, table_s, send, in_s, out_s, out_f,
-    local_sem, dec_sem, send_sem, recv_sem,
+    modes_s, table_s, send, in_s, mid_s, out_s, out_f,
+    local_sem, dec_sem, mid_sem, send_sem, recv_sem,
 ):
     lat, lon = lax.axis_index("lat"), lax.axis_index("lon")
     nlat = lax.axis_size("lat")
-    up, down = lax.rem(lat + nlat - 1, nlat), lax.rem(lat + 1, nlat)
     chans = modes_s.shape[3]
     mode_count = modes_s.shape[1]
 
@@ -86,25 +89,37 @@
         pltpu.make_async_copy(in_ref, in_s, local_sem.at[2]),
         pltpu.make_async_copy(out_ref, out_s, local_sem.at[3]),
     ]
+    middle = [
+        pltpu.make_async_copy(
+            mid_ref.at[a * 3 + b],
+            mid_s.at[a] if b == 1 else mid_v.at[3 * b // 2, a * CH : (a + 1) * CH],
+            mid_sem.at[a, b],
+        )
+        for a in range(3)
+        for b in range(3)
+    ]
     last = [
         pltpu.make_async_copy(
             dec_ref.at[k * chans : (k + 1) * chans], dec_v.at[k, 0:chans], dec_sem.at[k]
         )
         for k in range(NLON)
     ] + [
-        pltpu.make_async_copy(mid_ref, mid_v, local_sem.at[4]),
-        pltpu.make_async_copy(order_ref.at[lax.rem(lon, 2)], order_v, local_sem.at[5]),
+        pltpu.make_async_copy(order_ref.at[lax.rem(lon, 2)], order_v, local_sem.at[4]),
     ]
     for copy in early:
         copy.start()
     barrier = pltpu.get_barrier_semaphore()
-    for step in range(NLON):
-        there = lax.rem(lon + step, NLON)
-        for row in (up, down) if step == 0 else (up, down, lat):
-            pl.semaphore_signal(
-                barrier, inc=1, device_id={"lat": row, "lon": there}, device_id_type=MESH
-            )
-    for copy in late + last:
+
+    def greet(row, steps):
+        for step in steps:
+            there = {"lat": row, "lon": lax.rem(lon + step, NLON)}
+            pl.semaphore_signal(barrier, inc=1, device_id=there, device_id_type=MESH)
+
+    has_up, has_down = lat > 0, lat < nlat - 1
+    pl.when(has_up)(lambda: greet(lat - 1, range(NLON)))
+    pl.when(has_down)(lambda: greet(lat + 1, range(NLON)))
+    greet(lat, range(1, NLON))
+    for copy in late + middle + last:
         copy.start()
     send[...] = jnp.zeros_like(send)
     for copy in early:
@@ -116,36 +131,39 @@
         whole = (wide[:half] + wide[half:]).astype(BF16)
         send[:, row, :, 0:chans] = whole.reshape(NLON, TOK, chans)
     field[lon, 1:3] = send[lon]
-    pl.semaphore_wait(barrier, 3 * NLON - 1)
-    sends, receives = [], []
-    for step in range(NLON):
+    partners = NLON * (1 + has_up.astype(jnp.int32) + has_down.astype(jnp.int32)) - 1
+    pl.semaphore_wait(barrier, partners)
+
+    def transfer(way, step, mine):
         there = lax.rem(lon + step, NLON)
-        origin = lax.rem(lon + NLON - step, NLON)
-        for way, (row, source, target) in enumerate(
-            ((up, 0, 3), (down, 1, 0), (lat, None, None))
-        ):
-            if way == 2 and step == 0:
-                continue
-            copy = pltpu.make_async_remote_copy(
-                src_ref=send.at[there] if way == 2 else send.at[there, source],
-                dst_ref=field.at[lon, 1:3] if way == 2 else field.at[lon, target],
-                send_sem=send_sem.at[way, step],
-                recv_sem=recv_sem.at[way, step],
-                device_id={"lat": row, "lon": there},
-                device_id_type=MESH,
-            )
-            copy.start()
-            sends.append(copy)
-            receives.append(
-                pltpu.make_async_remote_copy(
-                    src_ref=send.at[there] if way == 2 else send.at[there, source],
-                    dst_ref=field.at[origin, 1:3] if way == 2 else field.at[origin, target],
-                    send_sem=send_sem.at[way, step],
-                    recv_sem=recv_sem.at[way, step],
-                    device_id={"lat": row, "lon": there},
-                    device_id_type=MESH,
-                )
-            )
+        owner = lon if mine else lax.rem(lon + NLON - step, NLON)
+        source = (send.at[there, 0], send.at[there, 1], send.at[there])[way]
+        target = (field.at[owner, 3], field.at[owner, 0], field.at[owner, 1:3])[way]
+        return pltpu.make_async_remote_copy(
+            src_ref=source,
+            dst_ref=target,
+            send_sem=send_sem.at[way, step],
+            recv_sem=recv_sem.at[way, step],
+            device_id={"lat": (lat - 1, lat + 1, lat)[way], "lon": there},
+            device_id_type=MESH,
+        )
+
+    def each(way, action, mine):
+        for step in range(1 if way == 2 else 0, NLON):
+            action(transfer(way, step, mine))
+
+    pl.when(has_up)(lambda: each(0, lambda copy: copy.start(), True))
+    pl.when(has_down)(lambda: each(1, lambda copy: copy.start(), True))
+    each(2, lambda copy: copy.start(), True)
+
+    @pl.when(jnp.logical_not(has_up))
+    def _():
+        field[:, 0] = jnp.zeros((NLON, TOK, 128), BF16)
+
+    @pl.when(jnp.logical_not(has_down))
+    def _():
+        field[:, 3] = jnp.zeros((NLON, TOK, 128), BF16)
+
     for copy in late:
         copy.wait()
     dec_v[:, chans:, :] = jnp.zeros((NLON, dec_v.shape[1] - chans, dec_v.shape[2]), BF16)
@@ -166,12 +184,22 @@
         for b in range(3):
             out_f[b * 8 + a : b * 8 + a + 1, :] = out_s[a, b : b + 1, :].astype(F32)
     out_v[...] = out_f[...].astype(BF16)
+    for copy in middle:
+        copy.wait()
+    for a in range(3):
+        here = slice(a * CH, (a + 1) * CH)
+        ends = mid_v[0, here].astype(F32) + mid_v[3, here].astype(F32)
+        centre = mid_s[a].astype(F32)
+        mid_v[1, here] = (0.5 * (ends + centre)).astype(BF16)
+        mid_v[2, here] = (0.5 * (ends - centre)).astype(BF16)
     for copy in last:
         copy.wait()
-    for copy in receives:
-        copy.wait_recv()
-    for copy in sends:
-        copy.wait_send()
+    pl.when(has_up)(lambda: each(1, lambda copy: copy.wait_recv(), False))
+    pl.when(has_down)(lambda: each(0, lambda copy: copy.wait_recv(), False))
+    each(2, lambda copy: copy.wait_recv(), False)
+    pl.when(has_up)(lambda: each(0, lambda copy: copy.wait_send(), True))
+    pl.when(has_down)(lambda: each(1, lambda copy: copy.wait_send(), True))
+    each(2, lambda copy: copy.wait_send(), True)
 
 
 def head_kernel(
@@ -183,9 +211,7 @@
     decoded = jnp.dot(
         flat, dec_v[...].reshape(NLON * 128, ROWL * PATCH), preferred_element_type=F32
     ).reshape(4, TQ, CG, ROWL * PATCH)
-    tokens[0] = jnp.where(top, 0.0, decoded[0])
-    tokens[1:3] = decoded[1:3]
-    tokens[3] = jnp.where(bottom, 0.0, decoded[3])
+    tokens[...] = decoded
 
     lane = lax.broadcasted_iota(jnp.int32, (CG, CH), 1)
 
@@ -228,33 +254,51 @@
         hidden = jnp.maximum(
             jnp.dot(window, in_v[j % 3], preferred_element_type=F32), 0.0
         ).reshape(WIN, SUB, 2 * CH)
-        for phase in range(2):
-            part = hidden[:, :, phase * CH : (phase + 1) * CH]
-            if j < 2:
-                part = jnp.where((side == 0) & top, 0.0, part)
-            if j >= RJ:
-                part = jnp.where((side == 1) & bottom, 0.0, part)
-            first[j, :, phase * SUB : (phase + 1) * SUB, :] = part.astype(BF16)
-
-    def mid_row(j, carry):
-        blocks = []
-        for a in range(3):
-            for b in range(3):
-                rows = first[j + a].reshape(PITCH, CH)
-                blocks.append(rows[b * SUB : b * SUB + T * SUB])
-        second = jnp.dot(
-            jnp.concatenate(blocks, axis=1), mid_v[...], preferred_element_type=F32
+        even, odd = hidden[:, :, :CH], hidden[:, :, CH:]
+        if j < 2:
+            even = jnp.where((side == 0) & top, 0.0, even)
+            odd = jnp.where((side == 0) & top, 0.0, odd)
+        if j >= RJ:
+            even = jnp.where((side == 1) & bottom, 0.0, even)
+            odd = jnp.where((side == 1) & bottom, 0.0, odd)
+        here = slice(j * STEP, (j + 1) * STEP)
+        first[0, here] = (even[:-1] - even[1:]).reshape(STEP, CH).astype(BF16)
+        first[1, here] = (odd[:-1] + even[1:]).reshape(STEP, CH).astype(BF16)
+        first[2, here] = (even[1:] - odd[:-1]).reshape(STEP, CH).astype(BF16)
+        first[3, here] = (odd[:-1] - odd[1:]).reshape(STEP, CH).astype(BF16)
+
+    for part in range(RJ // JB):
+        products = []
+        for k in range(4):
+            blocks = [
+                first[k, (part * JB + a) * STEP : (part * JB + a + JB) * STEP] for a in range(3)
+            ]
+            products.append(
+                jnp.dot(jnp.concatenate(blocks, axis=1), mid_v[k], preferred_element_type=F32)
+            )
+        pair = (
+            products[0] + (products[1] + products[2]),
+            (products[1] - products[2]) - products[3],
         )
-        second = jnp.maximum(second, 0.0).reshape(T, SUB, CH)
-        outside = ((side == 0) & top & (j == 0)) | ((side == 1) & bottom & (j == RJ - 1))
-        second = jnp.where(outside, 0.0, second).astype(BF16).reshape(T * SUB, CH)
-        tap = lax.dot_general(
-            out_v[...], second, (((1,), (1,)), ((), ())), preferred_element_type=F32
-        )
-        taps[j] = jnp.concatenate([tap[b * 8 : b * 8 + 8] for b in range(3)], axis=1)
-        return carry
-
-    lax.fori_loop(0, RJ, mid_row, 0)
+        pair = [jnp.maximum(x, 0.0).reshape(JB, PAIRS, SUB, CH) for x in pair]
+        for step in range(JB):
+            j = part * JB + step
+            seconds = []
+            for x in pair:
+                x = x[step]
+                if j == 0:
+                    x = jnp.where((side == 0) & top, 0.0, x)
+                if j == RJ - 1:
+                    x = jnp.where((side == 1) & bottom, 0.0, x)
+                seconds.append(x.reshape(STEP, CH).astype(BF16))
+            tap = lax.dot_general(
+                out_v[...],
+                jnp.concatenate(seconds, axis=0),
+                (((1,), (1,)), ((), ())),
+                preferred_element_type=F32,
+            )
+            taps[j] = jnp.concatenate([tap[b * 8 : b * 8 + 8] for b in range(3)], axis=1)
+
     tap = taps[...].reshape(RJ * 8, 3 * T * SUB)
     high = tap.astype(BF16)
     low = (tap - high.astype(F32)).astype(BF16)
@@ -284,7 +328,7 @@
             pltpu.VMEM((NLON, 4, TOK, 128), BF16),
             pltpu.VMEM((NLON, 128, ROWL * PATCH), BF16),
             pltpu.VMEM((3, CH, 2 * CH), BF16),
-            pltpu.VMEM((9 * CH, CH), BF16),
+            pltpu.VMEM((4, 3 * CH, CH), BF16),
             pltpu.VMEM((24, CH), BF16),
             pltpu.VMEM(order.shape[1:], BF16),
         ),
@@ -295,15 +339,17 @@
             pltpu.VMEM(table.shape, BF16),
             pltpu.VMEM((NLON, 2, TOK, 128), BF16),
             pltpu.VMEM(conv_in_weight.shape, BF16),
+            pltpu.VMEM((3, CH, CH), BF16),
             pltpu.VMEM((3, 3, CH), BF16),
             pltpu.VMEM((24, CH), F32),
-            dma((6,)),
+            dma((5,)),
             dma((NLON,)),
+            dma((3, 3)),
             dma((3, NLON)),
             dma((3, NLON)),
         ],
         compiler_params=pltpu.CompilerParams(
-            collective_id=0, has_side_effects=True, vmem_limit_bytes=24 * 2**20
+            has_side_effects=True, collective_id=0, vmem_limit_bytes=24 * 2**20
         ),
         name="exchange",
     )(
@@ -315,7 +361,7 @@
                 jnp.asarray(order),
                 decoder_weight,
                 conv_in_weight,
-                conv_mid_weight.reshape(9 * CH, CH),
+                conv_mid_weight.reshape(9, CH, CH),
                 conv_out_weight.reshape(3, 3, CH),
             )
         ]
@@ -329,7 +375,7 @@
         scratch_shapes=[
             pltpu.VMEM((4, TQ, CG, ROWL * PATCH), F32),
             pltpu.VMEM((PIX_J, WIN, SUB, CH), BF16),
-            pltpu.VMEM((FIRST_J, WIN, 2 * SUB, CH), BF16),
+            pltpu.VMEM((4, FIRST_J * STEP, CH), BF16),
             pltpu.VMEM((RJ, 8, 3 * T * SUB), F32),
             pltpu.VMEM((RJ * 8, RG * CH), F32),
         ],

time: 25.7 us -> 17.3 us (0.67)
  the two profiles are of different devices: /device:TPU:1 before, /device:TPU:128 now
where the time goes in v3:
time: 17.3 us; the launch traced here: 17.2 us
  Pallas kernels  17.2 us (99%)
    pallas_call x1, Pallas kernels, per_device(): pl.pallas_call(exchange_kernel, out_shape=(pltpu.VMEM((NLON, 4, TOK, 128)...  11.5 us
    pallas_call x1, Pallas kernels, per_device(): pl.pallas_call(head_kernel, out_shape=jax.ShapeDtypeStruct((ROWS, COLS),...  5.75 us

profile of v3, /device:TPU:128, one launch (start us, length us, event | category | flops | bytes accessed | tf_op | source)
XLA Modules:
  0.0 17.2 jit_solution(17939938992756912839)
XLA Ops:
  0.0 11.5 %exchange.1 = (bf16[8,4,24,128]{3,2,1,0:T(8,128)(2,1)S(1)}, bf16[8,128,1280]{2,1,0:T(8,128)(2,1)S(1)}, bf16[3,256,512]{2,1,0:T(8,128)(2,1)S(1)}, bf16[4,768,256]...) custom-call(bf16[2,90,2,96]{3,2,1,0:T(2,128)(2,1)} %modes_ref.1, ...), custom_call_target="tpu_custom_call" | custom-call | tf_op jit(solution)/shard_map/exchange/pallas_call | solution.py:325
  11.5 5.8 %head.1 = f32[16,180]{1,0:T(8,128)} custom-call(bf16[8,4,24,128]{3,2,1,0:T(8,128)(2,1)S(1)} %get-tuple-element.11.field, bf16[8,128,1280]{2,1,0:T(8,128)(2,1)S(1)} %get-tuple-element.12.dec_v, bf16[3,256,512]{2,1,0:T(8,128)(2,1)S(1)} %get-tuple-element.13.in_v, bf16[4,768,256]{2,1,0:T(8,128)(2,1)S(1)} %get-tuple-element.14.mid_v, ...), custom_call_target="tpu_custom_call" | custom-call | tf_op jit(solution)/shard_map/head/pallas_call | solution.py:370

commit v4 on v3

--- a/solution.py
+++ b/solution.py
@@ -18,6 +18,7 @@
 COLS = 180
 ROWS = 16
 OUT = 20
+FAR_FIRST = (2, 6, 1, 7, 3, 5, 4, 0)
 CH = 256
 TQ = 3
 CG = 8
@@ -28,7 +29,6 @@
 SUB = RG * CG
 FIRST_J = RJ + 2
 PIX_J = RJ + 4
-JB = 3
 WIN = (T + 2) // 2
 PAIRS = T // 2
 STEP = PAIRS * SUB
@@ -70,9 +70,10 @@
     return table.astype(BF16)
 
 
-def exchange_kernel(
+def field_kernel(
     modes_ref, table_ref, order_ref, dec_ref, in_ref, mid_ref, out_ref,
-    field, dec_v, in_v, mid_v, out_v, order_v,
+    taps, order_v,
+    field, dec_v, in_v, mid_v, out_v, tokens, pieces, first,
     modes_s, table_s, send, in_s, mid_s, out_s, out_f,
     local_sem, dec_sem, mid_sem, send_sem, recv_sem,
 ):
@@ -116,9 +117,12 @@
             pl.semaphore_signal(barrier, inc=1, device_id=there, device_id_type=MESH)
 
     has_up, has_down = lat > 0, lat < nlat - 1
-    pl.when(has_up)(lambda: greet(lat - 1, range(NLON)))
-    pl.when(has_down)(lambda: greet(lat + 1, range(NLON)))
-    greet(lat, range(1, NLON))
+    even = lax.rem(lat, 2) == 0
+    pl.when(even & has_up)(lambda: greet(lat - 1, FAR_FIRST))
+    pl.when(jnp.logical_not(even) & has_down)(lambda: greet(lat + 1, FAR_FIRST))
+    greet(lat, FAR_FIRST[:-1])
+    pl.when(even)(lambda: greet(lat + 1, FAR_FIRST))
+    pl.when(jnp.logical_not(even))(lambda: greet(lat - 1, FAR_FIRST))
     for copy in late + middle + last:
         copy.start()
     send[...] = jnp.zeros_like(send)
@@ -149,12 +153,17 @@
         )
 
     def each(way, action, mine):
-        for step in range(1 if way == 2 else 0, NLON):
+        for step in FAR_FIRST[:-1] if way == 2 else FAR_FIRST:
             action(transfer(way, step, mine))
 
-    pl.when(has_up)(lambda: each(0, lambda copy: copy.start(), True))
-    pl.when(has_down)(lambda: each(1, lambda copy: copy.start(), True))
-    each(2, lambda copy: copy.start(), True)
+    def begin(copy):
+        copy.start()
+
+    each(2, begin, True)
+    pl.when(even & has_up)(lambda: each(0, begin, True))
+    pl.when(jnp.logical_not(even) & has_down)(lambda: each(1, begin, True))
+    pl.when(even)(lambda: each(1, begin, True))
+    pl.when(jnp.logical_not(even))(lambda: each(0, begin, True))
 
     @pl.when(jnp.logical_not(has_up))
     def _():
@@ -192,26 +201,21 @@
         centre = mid_s[a].astype(F32)
         mid_v[1, here] = (0.5 * (ends + centre)).astype(BF16)
         mid_v[2, here] = (0.5 * (ends - centre)).astype(BF16)
-    for copy in last:
+    for copy in last[:NLON]:
         copy.wait()
-    pl.when(has_up)(lambda: each(1, lambda copy: copy.wait_recv(), False))
-    pl.when(has_down)(lambda: each(0, lambda copy: copy.wait_recv(), False))
     each(2, lambda copy: copy.wait_recv(), False)
-    pl.when(has_up)(lambda: each(0, lambda copy: copy.wait_send(), True))
-    pl.when(has_down)(lambda: each(1, lambda copy: copy.wait_send(), True))
-    each(2, lambda copy: copy.wait_send(), True)
-
-
-def head_kernel(
-    field, dec_v, in_v, mid_v, out_v, order_v, result, tokens, pieces, first, taps, sums
-):
-    lat = lax.axis_index("lat")
-    top, bottom = lat == 0, lat == lax.axis_size("lat") - 1
-    flat = jnp.concatenate([field[k].reshape(4 * TOK, 128) for k in range(NLON)], axis=1)
-    decoded = jnp.dot(
-        flat, dec_v[...].reshape(NLON * 128, ROWL * PATCH), preferred_element_type=F32
-    ).reshape(4, TQ, CG, ROWL * PATCH)
-    tokens[...] = decoded
+
+    top, bottom = jnp.logical_not(has_up), jnp.logical_not(has_down)
+    weights = dec_v.reshape(NLON * 128, ROWL * PATCH)
+
+    def decode(low, high, start, stop):
+        count = high - low
+        values = jnp.concatenate(
+            [field[k, low:high].reshape(count * TOK, 128) for k in range(NLON)], axis=1
+        )
+        tokens[low:high, :, :, start:stop] = jnp.dot(
+            values, weights[:, start:stop], preferred_element_type=F32
+        ).reshape(count, TQ, CG, stop - start)
 
     lane = lax.broadcasted_iota(jnp.int32, (CG, CH), 1)
 
@@ -221,58 +225,55 @@
         shift = (place - (start - base)) % CH
         return pltpu.roll(block, shift, 1) if shift else block
 
-    halves = {}
-    for p in range(-3, 19):
+    def half(p, w):
         slot, pr, place = p // PATCH + 1, p % PATCH, p % 3 * 80
-        for w in range(WIN - 1):
-            tq, part = divmod(w, 4)
-            if part:
-                value = placed(slot, tq, pr * ROWL + (part - 1) * 40, place)
-            else:
-                before = placed(slot, (tq - 1) % TQ, pr * ROWL + 120, place)
-                if tq == 0:
-                    before = pltpu.roll(before, 1, 0)
-                own = placed(slot, tq, pr * ROWL, place + 40)
-                value = jnp.where(lane < place + 40, before, own)
-            halves[p, w] = value
-        before = placed(slot, TQ - 1, pr * ROWL + 120, place)
-        after = pltpu.roll(placed(slot, 0, pr * ROWL, place + 40), CG - 1, 0)
-        halves[p, WIN - 1] = jnp.where(lane < place + 40, before, after)
-        if p >= 6:
+        tq, part = divmod(w, 4)
+        if part:
+            return placed(slot, tq, pr * ROWL + (part - 1) * 40, place)
+        before = placed(slot, (tq - 1) % TQ, pr * ROWL + 120, place)
+        own = placed(slot, tq % TQ, pr * ROWL, place + 40)
+        if tq == 0:
+            before = pltpu.roll(before, 1, 0)
+        if tq == TQ:
+            own = pltpu.roll(own, CG - 1, 0)
+        return jnp.where(lane < place + 40, before, own)
+
+    def spread(rows):
+        for i in rows:
             for w in range(WIN):
-                pieces[p - 6, w] = jnp.concatenate(
-                    [halves.pop((p - 9, w)), halves[p, w]], axis=0
+                pieces[i, w] = jnp.concatenate(
+                    [half(i - 3, w), half(i - 3 + RJ, w)], axis=0
                 ).astype(BF16)
 
     lane2 = lax.broadcasted_iota(jnp.int32, (SUB, CH), 1)
     side = lax.broadcasted_iota(jnp.int32, (SUB, CH), 0) // CG
-    for j in range(FIRST_J):
-        ordered = [pieces[j + (c - j) % 3] for c in range(3)]
-        window = jnp.where(
-            lane2 < 80, ordered[0], jnp.where(lane2 < 160, ordered[1], ordered[2])
-        ).reshape(WIN * SUB, CH)
-        hidden = jnp.maximum(
-            jnp.dot(window, in_v[j % 3], preferred_element_type=F32), 0.0
-        ).reshape(WIN, SUB, 2 * CH)
-        even, odd = hidden[:, :, :CH], hidden[:, :, CH:]
-        if j < 2:
-            even = jnp.where((side == 0) & top, 0.0, even)
-            odd = jnp.where((side == 0) & top, 0.0, odd)
-        if j >= RJ:
-            even = jnp.where((side == 1) & bottom, 0.0, even)
-            odd = jnp.where((side == 1) & bottom, 0.0, odd)
-        here = slice(j * STEP, (j + 1) * STEP)
-        first[0, here] = (even[:-1] - even[1:]).reshape(STEP, CH).astype(BF16)
-        first[1, here] = (odd[:-1] + even[1:]).reshape(STEP, CH).astype(BF16)
-        first[2, here] = (even[1:] - odd[:-1]).reshape(STEP, CH).astype(BF16)
-        first[3, here] = (odd[:-1] - odd[1:]).reshape(STEP, CH).astype(BF16)
-
-    for part in range(RJ // JB):
+
+    def first_rows(rows):
+        for j in rows:
+            ordered = [pieces[j + (c - j) % 3] for c in range(3)]
+            window = jnp.where(
+                lane2 < 80, ordered[0], jnp.where(lane2 < 160, ordered[1], ordered[2])
+            ).reshape(WIN * SUB, CH)
+            hidden = jnp.maximum(
+                jnp.dot(window, in_v[j % 3], preferred_element_type=F32), 0.0
+            ).reshape(WIN, SUB, 2 * CH)
+            left, right = hidden[:, :, :CH], hidden[:, :, CH:]
+            if j < 2:
+                left = jnp.where((side == 0) & top, 0.0, left)
+                right = jnp.where((side == 0) & top, 0.0, right)
+            if j >= RJ:
+                left = jnp.where((side == 1) & bottom, 0.0, left)
+                right = jnp.where((side == 1) & bottom, 0.0, right)
+            here = slice(j * STEP, (j + 1) * STEP)
+            first[0, here] = (left[:-1] - left[1:]).reshape(STEP, CH).astype(BF16)
+            first[1, here] = (right[:-1] + left[1:]).reshape(STEP, CH).astype(BF16)
+            first[2, here] = (left[1:] - right[:-1]).reshape(STEP, CH).astype(BF16)
+            first[3, here] = (right[:-1] - right[1:]).reshape(STEP, CH).astype(BF16)
+
+    def second_rows(low, count):
         products = []
         for k in range(4):
-            blocks = [
-                first[k, (part * JB + a) * STEP : (part * JB + a + JB) * STEP] for a in range(3)
-            ]
+            blocks = [first[k, (low + a) * STEP : (low + a + count) * STEP] for a in range(3)]
             products.append(
                 jnp.dot(jnp.concatenate(blocks, axis=1), mid_v[k], preferred_element_type=F32)
             )
@@ -280,9 +281,9 @@
             products[0] + (products[1] + products[2]),
             (products[1] - products[2]) - products[3],
         )
-        pair = [jnp.maximum(x, 0.0).reshape(JB, PAIRS, SUB, CH) for x in pair]
-        for step in range(JB):
-            j = part * JB + step
+        pair = [jnp.maximum(x, 0.0).reshape(count, PAIRS, SUB, CH) for x in pair]
+        for step in range(count):
+            j = low + step
             seconds = []
             for x in pair:
                 x = x[step]
@@ -299,6 +300,28 @@
             )
             taps[j] = jnp.concatenate([tap[b * 8 : b * 8 + 8] for b in range(3)], axis=1)
 
+    decode(1, 3, 0, ROWL * PATCH)
+    spread(range(3, 10))
+    first_rows(range(3, 8))
+    second_rows(3, 3)
+
+    pl.when(has_up)(lambda: each(1, lambda copy: copy.wait_recv(), False))
+    pl.when(has_down)(lambda: each(0, lambda copy: copy.wait_recv(), False))
+    decode(0, 1, 768, ROWL * PATCH)
+    decode(3, 4, 0, 512)
+    spread((0, 1, 2, 10, 11, 12))
+    first_rows((0, 1, 2, 8, 9, 10))
+    second_rows(0, 3)
+    second_rows(6, 3)
+
+    for copy in last[NLON:]:
+        copy.wait()
+    pl.when(has_up)(lambda: each(0, lambda copy: copy.wait_send(), True))
+    pl.when(has_down)(lambda: each(1, lambda copy: copy.wait_send(), True))
+    each(2, lambda copy: copy.wait_send(), True)
+
+
+def order_kernel(taps, order_v, result, sums):
     tap = taps[...].reshape(RJ * 8, 3 * T * SUB)
     high = tap.astype(BF16)
     low = (tap - high.astype(F32)).astype(BF16)
@@ -320,21 +343,24 @@
     table = dft_table(mode_count)
     order = order_table()
     vmem = pl.BlockSpec(memory_space=pltpu.VMEM)
-    anywhere = pl.BlockSpec(memory_space=pltpu.HBM)
     dma = pltpu.SemaphoreType.DMA
     staged = pl.pallas_call(
-        exchange_kernel,
+        field_kernel,
         out_shape=(
+            pltpu.VMEM((RJ, 8, 3 * T * SUB), F32),
+            pltpu.VMEM(order.shape[1:], BF16),
+        ),
+        in_specs=[pl.BlockSpec(memory_space=pltpu.HBM)] * 7,
+        out_specs=(vmem,) * 2,
+        scratch_shapes=[
             pltpu.VMEM((NLON, 4, TOK, 128), BF16),
             pltpu.VMEM((NLON, 128, ROWL * PATCH), BF16),
             pltpu.VMEM((3, CH, 2 * CH), BF16),
             pltpu.VMEM((4, 3 * CH, CH), BF16),
             pltpu.VMEM((24, CH), BF16),
-            pltpu.VMEM(order.shape[1:], BF16),
-        ),
-        in_specs=[anywhere] * 7,
-        out_specs=(vmem,) * 6,
-        scratch_shapes=[
+            pltpu.VMEM((4, TQ, CG, ROWL * PATCH), F32),
+            pltpu.VMEM((PIX_J, WIN, SUB, CH), BF16),
+            pltpu.VMEM((4, FIRST_J * STEP, CH), BF16),
             pltpu.VMEM(kept_modes.shape, BF16),
             pltpu.VMEM(table.shape, BF16),
             pltpu.VMEM((NLON, 2, TOK, 128), BF16),
@@ -349,9 +375,9 @@
             dma((3, NLON)),
         ],
         compiler_params=pltpu.CompilerParams(
-            has_side_effects=True, collective_id=0, vmem_limit_bytes=24 * 2**20
+            collective_id=0, has_side_effects=True, vmem_limit_bytes=40 * 2**20
         ),
-        name="exchange",
+        name="field_to_taps",
     )(
         *[
             pltpu.with_memory_space_constraint(x, pltpu.HBM)
@@ -368,19 +394,13 @@
     )
     staged = [pltpu.with_memory_space_constraint(x, pltpu.VMEM) for x in staged]
     return pl.pallas_call(
-        head_kernel,
+        order_kernel,
         out_shape=jax.ShapeDtypeStruct((ROWS, COLS), F32),
-        in_specs=[vmem] * 6,
+        in_specs=[vmem] * 2,
         out_specs=vmem,
-        scratch_shapes=[
-            pltpu.VMEM((4, TQ, CG, ROWL * PATCH), F32),
-            pltpu.VMEM((PIX_J, WIN, SUB, CH), BF16),
-            pltpu.VMEM((4, FIRST_J * STEP, CH), BF16),
-            pltpu.VMEM((RJ, 8, 3 * T * SUB), F32),
-            pltpu.VMEM((RJ * 8, RG * CH), F32),
-        ],
-        compiler_params=pltpu.CompilerParams(vmem_limit_bytes=32 * 2**20),
-        name="head",
+        scratch_shapes=[pltpu.VMEM((RJ * 8, RG * CH), F32)],
+        compiler_params=pltpu.CompilerParams(vmem_limit_bytes=16 * 2**20),
+        name="order",
     )(*staged)
 
 

time: 17.3 us -> 16.8 us (0.971)
  the two profiles are of different devices: /device:TPU:128 before, /device:TPU:103 now
where the time goes in v4:
time: 16.8 us; the launch traced here: 16.5 us
  Pallas kernels  16.5 us (98%)
    pallas_call x1, Pallas kernels, per_device(): pl.pallas_call(field_kernel, out_shape=(pltpu.VMEM((RJ, 8, 3 * T * SUB),...  15.4 us
    pallas_call x1, Pallas kernels, per_device(): pl.pallas_call(order_kernel, out_shape=jax.ShapeDtypeStruct((ROWS, COLS),...  1 us

profile of v4, /device:TPU:103, one launch (start us, length us, event | category | flops | bytes accessed | tf_op | source)
XLA Modules:
  0.0 16.5 jit_solution(14911265389397677709)
XLA Ops:
  0.0 15.4 %field_to_taps.1 = (f32[9,8,1152]{2,1,0:T(8,128)S(1)}, bf16[1152,512]{1,0:T(8,128)(2,1)S(1)}) custom-call(bf16[2,90,2,96]{3,2,1,0:T(2,128)(2,1)} %modes_ref.1, bf16[384,180]{1,0:T(8,128)(2,1)} %constant.4.clone.table_ref, bf16[2,1152,512]{2,1,0:T(8,128)(2,1)} %constant.5.clone.order_ref, bf16[768,1280]{1,0:T(8,128)(2,1)} %dec_ref.1, ...), custom_call_target="tpu_custom_call" | custom-call | tf_op jit(solution)/shard_map/field_to_taps/pallas_call | solution.py:347
  15.5 1.0 %order.1 = f32[16,180]{1,0:T(8,128)} custom-call(f32[9,8,1152]{2,1,0:T(8,128)S(1)} %get-tuple-element.7.taps, bf16[1152,512]{1,0:T(8,128)(2,1)S(1)} %get-tuple-element.8.order_v), custom_call_target="tpu_custom_call" | custom-call | tf_op jit(solution)/shard_map/order/pallas_call | solution.py:396

commit v5 on v4

v5 whole, which is shorter than its diff:
```python
import math

import jax
import jax.numpy as jnp
import numpy as np
from jax import lax
from jax.experimental import pallas as pl
from jax.experimental.pallas import tpu as pltpu
from jax.sharding import PartitionSpec as P

MESH = pl.DeviceIdType.MESH
BF16 = jnp.bfloat16
F32 = jnp.float32

LON_TOK = 180
PATCH = 8
NLON = 8
COLS = 180
ROWS = 16
OUT = 20
FAR_FIRST = (2, 6, 1, 7, 3, 5, 4, 0)
CH = 256
TQ = 3
CG = 8
TOK = TQ * CG
SIDES = 2
T = TQ * PATCH // SIDES
SUB = SIDES * CG
WIN = (T + 2) // 2
PAIRS = T // 2
STEP = PAIRS * SUB
SECOND = ROWS + 2
FIRST = ROWS + 4
PIX = ROWS + 6
SECOND_ORDER = tuple(range(3, 15)) + (0, 1, 2, 15, 16, 17)
ROWL = PATCH * OUT
EDGE = 512


def first_token(sector):
    return (COLS * sector - 3) // PATCH


def dft_table(mode_count):
    ids = []
    for d in range(NLON):
        for tq in range(TQ):
            for cg in range(CG):
                ids.append((first_token(d) + cg * TQ + tq) % LON_TOK)
    modes = np.arange(mode_count)
    angle = (np.array(ids)[:, None] * modes[None, :] % LON_TOK) * (2.0 * math.pi / LON_TOK)
    scale = np.where(modes == 0, 1.0, 2.0) / math.sqrt(LON_TOK)
    table = np.stack([scale * np.cos(angle), -scale * np.sin(angle)], axis=2)
    table = table.reshape(len(ids), 2 * mode_count).astype(np.float32)
    high = table.astype(BF16)
    low = (table - high.astype(np.float32)).astype(BF16)
    return np.concatenate([high, low], axis=0)


def order_table():
    table = np.zeros((2, 3 * 4 * STEP, 2 * CH), np.float32)
    for parity in range(2):
        offset = COLS * parity - PATCH * first_token(parity)
        for b in range(3):
            for q in range(COLS):
                cg, rest = divmod(q + offset - 1 + b, T * SIDES)
                side, t = divmod(rest, T)
                pair, phase = divmod(t, 2)
                at = (b * 4 + phase) * STEP + pair * SUB + side * CG + cg
                for row in range(2):
                    table[parity, at + row * 2 * STEP, row * CH + q] = 1.0
    return table.astype(BF16)


def field_kernel(
    modes_ref, table_ref, order_ref, dec_ref, in_ref, mid_ref, out_ref,
    taps, order_v,
    field, edges, halo, dec_v, in_v, mid_v, out_v, tokens, pieces, first,
    modes_s, table_s, send, in_s, mid_s, out_s, out_f,
    local_sem, dec_sem, mid_sem, send_sem, recv_sem, ready,
):
    lat, lon = lax.axis_index("lat"), lax.axis_index("lon")
    nlat = lax.axis_size("lat")
    chans = modes_s.shape[3]
    mode_count = modes_s.shape[1]

    early = [
        pltpu.make_async_copy(modes_ref, modes_s, local_sem.at[0]),
        pltpu.make_async_copy(table_ref, table_s, local_sem.at[1]),
    ]
    late = [
        pltpu.make_async_copy(in_ref, in_s, local_sem.at[2]),
        pltpu.make_async_copy(out_ref, out_s, local_sem.at[3]),
    ]
    middle = [
        pltpu.make_async_copy(
            mid_ref.at[a * 3 + b],
            mid_s.at[a] if b == 1 else mid_v.at[3 * b // 2, a * CH : (a + 1) * CH],
            mid_sem.at[a, b],
        )
        for a in range(3)
        for b in range(3)
    ]
    last = [
        pltpu.make_async_copy(
            dec_ref.at[k * chans : (k + 1) * chans], dec_v.at[k, 0:chans], dec_sem.at[k]
        )
        for k in range(NLON)
    ] + [
        pltpu.make_async_copy(order_ref.at[lax.rem(lon, 2)], order_v, local_sem.at[4]),
    ]
    for copy in early:
        copy.start()
    barrier = pltpu.get_barrier_semaphore()

    odd = lax.rem(lat, 2)
    near = lat + 1 - 2 * odd
    far = lat - 1 + 2 * odd
    has_far = (far >= 0) & (far < nlat)

    greets, greeted = has_far & (odd == 1), has_far & (odd == 0)

    def greet(semaphore, row, column):
        there = {"lat": row, "lon": column}
        pl.semaphore_signal(semaphore, inc=1, device_id=there, device_id_type=MESH)

    pl.when(greets)(lambda: greet(barrier, far, lon))
    for step in FAR_FIRST[:-1]:
        greet(barrier, lat, lax.rem(lon + step, NLON))
    greet(barrier, near, lon)
    for copy in late + middle + last:
        copy.start()
    send[...] = jnp.zeros_like(send)
    for copy in early:
        copy.wait()
    for row in range(2):
        values = modes_s[row].reshape(2 * mode_count, chans)
        wide = jnp.dot(table_s[...], values, preferred_element_type=F32)
        half = wide.shape[0] // 2
        whole = (wide[:half] + wide[half:]).astype(BF16)
        send[:, row, :, 0:chans] = whole.reshape(NLON, TOK, chans)
    for row in range(2):
        field[row, lon] = send[lon, row]
    pl.semaphore_wait(barrier, NLON + greeted.astype(jnp.int32))
    pl.when(greeted)(lambda: greet(ready, far, lon))

    def across(step, mine):
        there = lax.rem(lon + step, NLON)
        owner = lon if mine else lax.rem(lon + NLON - step, NLON)
        return pltpu.make_async_remote_copy(
            src_ref=send.at[there],
            dst_ref=field.at[:, owner],
            send_sem=send_sem.at[step],
            recv_sem=recv_sem.at[step],
            device_id={"lat": lat, "lon": there},
            device_id_type=MESH,
        )

    def onward(way, row, source, target):
        return pltpu.make_async_remote_copy(
            src_ref=edges.at[source],
            dst_ref=halo.at[target],
            send_sem=send_sem.at[NLON + way],
            recv_sem=recv_sem.at[NLON + way],
            device_id={"lat": row, "lon": lon},
            device_id_type=MESH,
        )

    to_near, from_near = (onward(0, near, 1 - odd, slot) for slot in (odd, 1 - odd))
    to_far, from_far = (onward(1, far, odd, slot) for slot in (1 - odd, odd))

    for step in FAR_FIRST[:-1]:
        across(step, True).start()

    @pl.when(jnp.logical_not(has_far))
    def _():
        halo[odd] = jnp.zeros(halo.shape[1:], BF16)

    for copy in late:
        copy.wait()
    dec_v[:, chans:, :] = jnp.zeros((NLON, dec_v.shape[1] - chans, dec_v.shape[2]), BF16)
    for turn in range(3):
        for phase in range(2):
            rows = []
            for place in range(3):
                a = (place - turn) % 3
                if phase:
                    rows.append(jnp.zeros((OUT, CH), BF16))
                rows += [in_s[a, b] for b in range(3)]
                if not phase:
                    rows.append(jnp.zeros((OUT, CH), BF16))
            rows.append(jnp.zeros((16, CH), BF16))
            in_v[turn, :, phase * CH : (phase + 1) * CH] = jnp.concatenate(rows, axis=0)
    out_f[...] = jnp.zeros_like(out_f)
    for a in range(3):
        for b in range(3):
            out_f[b * 8 + a : b * 8 + a + 1, :] = out_s[a, b : b + 1, :].astype(F32)
    out_v[...] = out_f[...].astype(BF16)
    for copy in middle:
        copy.wait()
    for a in range(3):
        here = slice(a * CH, (a + 1) * CH)
        ends = mid_v[0, here].astype(F32) + mid_v[3, here].astype(F32)
        centre = mid_s[a].astype(F32)
        mid_v[1, here] = (0.5 * (ends + centre)).astype(BF16)
        mid_v[2, here] = (0.5 * (ends - centre)).astype(BF16)
    for copy in last[:NLON]:
        copy.wait()
    for step in FAR_FIRST[:-1]:
        across(step, False).wait_recv()
    top, bottom = lat == 0, lat == nlat - 1
    weights = dec_v[...].reshape(NLON * 128, ROWL * PATCH)

    values = jnp.concatenate([field[:, k].reshape(2 * TOK, 128) for k in range(NLON)], axis=1)
    pixels = jnp.dot(values, weights, preferred_element_type=F32)
    edges[0] = pixels[:TOK, :EDGE].astype(BF16)
    edges[1] = pixels[TOK:, -EDGE:].astype(BF16)

    @pl.when(has_far)
    def _():
        pl.when(greets)(lambda: pl.semaphore_wait(ready, 1))
        to_far.start()

    to_near.start()
    tokens[1:3] = pixels.reshape(2, TQ, CG, ROWL * PATCH)

    lane = lax.broadcasted_iota(jnp.int32, (CG, CH), 1)

    def placed(slot, tq, start, place):
        base = min(start // 128 * 128, ROWL * PATCH - CH)
        block = tokens[slot, tq, :, base : base + CH]
        shift = (place - (start - base)) % CH
        return pltpu.roll(block, shift, 1) if shift else block

    def half(p, w):
        slot, pr, place = p // PATCH + 1, p % PATCH, p % 3 * 80
        tq, part = divmod(w, 4)
        if part:
            return placed(slot, tq, pr * ROWL + (part - 1) * 40, place)
        before = placed(slot, (tq - 1) % TQ, pr * ROWL + 120, place)
        own = placed(slot, tq % TQ, pr * ROWL, place + 40)
        if tq == 0:
            before = pltpu.roll(before, 1, 0)
        if tq == TQ:
            own = pltpu.roll(own, CG - 1, 0)
        return jnp.where(lane < place + 40, before, own)

    def spread(rows):
        for i in rows:
            values = [half(i - 3, w) for w in range(SIDES * PAIRS + 1)]
            for w in range(WIN):
                pieces[i, w] = jnp.concatenate([values[w], values[w + PAIRS]], axis=0).astype(BF16)

    lane2 = lax.broadcasted_iota(jnp.int32, (SUB, CH), 1)

    def first_rows(rows):
        for turn in range(3):
            mine = [j for j in rows if j % 3 == turn]
            windows = []
            for j in mine:
                parts = [pieces[j + (c - j) % 3] for c in range(3)]
                window = jnp.where(lane2 < 80, parts[0], jnp.where(lane2 < 160, parts[1], parts[2]))
                windows.append(window.reshape(WIN * SUB, CH))
            hidden = jnp.maximum(
                jnp.dot(
                    jnp.concatenate(windows, axis=0), in_v[turn], preferred_element_type=F32
                ),
                0.0,
            ).reshape(len(mine), WIN, SUB, 2 * CH)
            for at, j in enumerate(mine):
                left, right = hidden[at, :, :, :CH], hidden[at, :, :, CH:]
                if j < 2 or j >= FIRST - 2:
                    outside = top if j < 2 else bottom
                    left = jnp.where(outside, 0.0, left)
                    right = jnp.where(outside, 0.0, right)
                here = slice(j * STEP, (j + 1) * STEP)
                first[0, here] = (left[:-1] - left[1:]).reshape(STEP, CH).astype(BF16)
                first[1, here] = (right[:-1] + left[1:]).reshape(STEP, CH).astype(BF16)
                first[2, here] = (left[1:] - right[:-1]).reshape(STEP, CH).astype(BF16)
                first[3, here] = (right[:-1] - right[1:]).reshape(STEP, CH).astype(BF16)

    def second_rows(low, count):
        products = []
        for k in range(4):
            blocks = [first[k, (low + a) * STEP : (low + a + count) * STEP] for a in range(3)]
            products.append(
                jnp.dot(jnp.concatenate(blocks, axis=1), mid_v[k], preferred_element_type=F32)
            )
        pair = (
            products[0] + (products[1] + products[2]),
            (products[1] - products[2]) - products[3],
        )
        pair = [jnp.maximum(x, 0.0).reshape(count, STEP, CH) for x in pair]
        rows = []
        for step in range(count):
            values = [x[step] for x in pair]
            if low + step == 0:
                values = [jnp.where(top, 0.0, x) for x in values]
            if low + step == SECOND - 1:
                values = [jnp.where(bottom, 0.0, x) for x in values]
            rows += [x.astype(BF16) for x in values]
        return rows

    def last_taps(rows, slot):
        for i in range(0, len(rows), 4):
            tap = lax.dot_general(
                out_v[...],
                jnp.concatenate(rows[i : i + 4], axis=0),
                (((1,), (1,)), ((), ())),
                preferred_element_type=F32,
            )
            taps[slot + i // 4] = jnp.concatenate([tap[b * 8 : b * 8 + 8] for b in range(3)], axis=1)

    spread(range(3, 19))
    first_rows(range(3, 17))
    last_taps(second_rows(3, 6), 0)
    last_taps(second_rows(9, 6), 3)

    from_near.wait_recv()
    pl.when(has_far)(lambda: from_far.wait_recv())
    tokens[0, :, :, -EDGE:] = halo[0].astype(F32).reshape(TQ, CG, EDGE)
    tokens[3, :, :, :EDGE] = halo[1].astype(F32).reshape(TQ, CG, EDGE)
    spread((0, 1, 2, 19, 20, 21))
    first_rows((0, 1, 2, 17, 18, 19))
    last_taps(second_rows(0, 3) + second_rows(15, 3), 6)

    for copy in last[NLON:]:
        copy.wait()
    for step in FAR_FIRST[:-1]:
        across(step, True).wait_send()
    to_near.wait_send()
    pl.when(has_far)(lambda: to_far.wait_send())


def order_kernel(taps, order_v, result, sums):
    count = taps.shape[0] * 8
    tap = taps[...].reshape(count, 3 * 4 * STEP)
    high = tap.astype(BF16)
    low = (tap - high.astype(F32)).astype(BF16)
    moved = jnp.dot(
        jnp.concatenate([high, low], axis=0), order_v[...], preferred_element_type=F32
    )
    sums[...] = moved[:count] + moved[count:]
    for p in range(ROWS):
        total = None
        for a in range(3):
            slot, half = divmod(SECOND_ORDER.index(p + a), 2)
            term = sums[slot * 8 + a : slot * 8 + a + 1, half * CH : half * CH + COLS]
            total = term if total is None else total + term
        result[p : p + 1, :] = total


def per_device(kept_modes, decoder_weight, conv_in_weight, conv_mid_weight, conv_out_weight):
    mode_count, chans = kept_modes.shape[1], kept_modes.shape[3]
    table = dft_table(mode_count)
    order = order_table()
    vmem = pl.BlockSpec(memory_space=pltpu.VMEM)
    dma = pltpu.SemaphoreType.DMA
    staged = pl.pallas_call(
        field_kernel,
        out_shape=(
            pltpu.VMEM((SECOND // 2, 8, 3 * 4 * STEP), F32),
            pltpu.VMEM(order.shape[1:], BF16),
        ),
        in_specs=[pl.BlockSpec(memory_space=pltpu.HBM)] * 7,
        out_specs=(vmem,) * 2,
        scratch_shapes=[
            pltpu.VMEM((2, NLON, TOK, 128), BF16),
            pltpu.VMEM((2, TOK, EDGE), BF16),
            pltpu.VMEM((2, TOK, EDGE), BF16),
            pltpu.VMEM((NLON, 128, ROWL * PATCH), BF16),
            pltpu.VMEM((3, CH, 2 * CH), BF16),
            pltpu.VMEM((4, 3 * CH, CH), BF16),
            pltpu.VMEM((24, CH), BF16),
            pltpu.VMEM((4, TQ, CG, ROWL * PATCH), F32),
            pltpu.VMEM((PIX, WIN, SUB, CH), BF16),
            pltpu.VMEM((4, FIRST * STEP, CH), BF16),
            pltpu.VMEM(kept_modes.shape, BF16),
            pltpu.VMEM(table.shape, BF16),
            pltpu.VMEM((NLON, 2, TOK, 128), BF16),
            pltpu.VMEM(conv_in_weight.shape, BF16),
            pltpu.VMEM((3, CH, CH), BF16),
            pltpu.VMEM((3, 3, CH), BF16),
            pltpu.VMEM((24, CH), F32),
            dma((5,)),
            dma((NLON,)),
            dma((3, 3)),
            dma((NLON + 2,)),
            dma((NLON + 2,)),
            pltpu.SemaphoreType.REGULAR,
        ],
        compiler_params=pltpu.CompilerParams(
            collective_id=0, has_side_effects=True, vmem_limit_bytes=40 * 2**20
        ),
        name="field_to_taps",
    )(
        *[
            pltpu.with_memory_space_constraint(x, pltpu.HBM)
            for x in (
                kept_modes,
                jnp.asarray(table),
                jnp.asarray(order),
                decoder_weight,
                conv_in_weight,
                conv_mid_weight.reshape(9, CH, CH),
                conv_out_weight.reshape(3, 3, CH),
            )
        ]
    )
    staged = [pltpu.with_memory_space_constraint(x, pltpu.VMEM) for x in staged]
    return pl.pallas_call(
        order_kernel,
        out_shape=jax.ShapeDtypeStruct((ROWS, COLS), F32),
        in_specs=[vmem] * 2,
        out_specs=vmem,
        scratch_shapes=[pltpu.VMEM((SECOND // 2 * 8, 2 * CH), F32)],
        compiler_params=pltpu.CompilerParams(vmem_limit_bytes=16 * 2**20),
        name="order",
    )(*staged)


def solution(mesh):
    placed = (P("lat", None, None, "lon"), P(), P(), P(), P())
    return jax.shard_map(
        per_device, mesh=mesh, in_specs=placed, out_specs=P("lat", "lon"), check_vma=False
    )
```

time: 16.8 us -> 16.5 us (0.982); the launches traced: 16.5 us -> 16.5 us
  no operation moved by 1% of the time
where the time goes in v5:
time: 16.5 us
  Pallas kernels  16.5 us (100%)
    pallas_call x1, Pallas kernels, per_device(): pl.pallas_call(field_kernel, out_shape=(pltpu.VMEM((SECOND // 2, 8, 3 * 4...  15.5 us
    pallas_call x1, Pallas kernels, per_device(): pl.pallas_call(order_kernel, out_shape=jax.ShapeDtypeStruct((ROWS, COLS),...  1 us

profile of v5, /device:TPU:103, one launch (start us, length us, event | category | flops | bytes accessed | tf_op | source)
XLA Modules:
  0.0 16.5 jit_solution(8998928255667831307)
XLA Ops:
  0.0 15.5 %field_to_taps.1 = (f32[9,8,1152]{2,1,0:T(8,128)S(1)}, bf16[1152,512]{1,0:T(8,128)(2,1)S(1)}) custom-call(bf16[2,90,2,96]{3,2,1,0:T(2,128)(2,1)} %modes_ref.1, bf16[384,180]{1,0:T(8,128)(2,1)} %constant.4.clone.table_ref, bf16[2,1152,512]{2,1,0:T(8,128)(2,1)} %constant.5.clone.order_ref, bf16[768,1280]{1,0:T(8,128)(2,1)} %dec_ref.1, ...), custom_call_target="tpu_custom_call" | custom-call | tf_op jit(solution)/shard_map/field_to_taps/pallas_call | solution.py:359
  15.5 1.0 %order.1 = f32[16,180]{1,0:T(8,128)} custom-call(f32[9,8,1152]{2,1,0:T(8,128)S(1)} %get-tuple-element.7.taps, bf16[1152,512]{1,0:T(8,128)(2,1)S(1)} %get-tuple-element.8.order_v), custom_call_target="tpu_custom_call" | custom-call | tf_op jit(solution)/shard_map/order/pallas_call | solution.py:411

commit v6 on v5

--- a/solution.py
+++ b/solution.py
@@ -75,7 +75,7 @@
 def field_kernel(
     modes_ref, table_ref, order_ref, dec_ref, in_ref, mid_ref, out_ref,
     taps, order_v,
-    field, edges, halo, dec_v, in_v, mid_v, out_v, tokens, pieces, first,
+    field, edges, halo, beyond, dec_v, in_v, mid_v, out_v, tokens, pieces, first,
     modes_s, table_s, send, in_s, mid_s, out_s, out_f,
     local_sem, dec_sem, mid_sem, send_sem, recv_sem, ready,
 ):
@@ -118,13 +118,20 @@
     far = lat - 1 + 2 * odd
     has_far = (far >= 0) & (far < nlat)
 
-    greets, greeted = has_far & (odd == 1), has_far & (odd == 0)
+    upper = jnp.minimum(lat, far)
+    swap = (lax.rem(upper, 4) == 3) & (upper >= nlat // 2)
+    leads = (odd == 1) != swap
+    greets, greeted = has_far & leads, has_far & jnp.logical_not(leads)
 
     def greet(semaphore, row, column):
         there = {"lat": row, "lon": column}
         pl.semaphore_signal(semaphore, inc=1, device_id=there, device_id_type=MESH)
 
-    pl.when(greets)(lambda: greet(barrier, far, lon))
+    @pl.when(greets)
+    def _():
+        for step in FAR_FIRST:
+            greet(barrier, far, lax.rem(lon + step, NLON))
+
     for step in FAR_FIRST[:-1]:
         greet(barrier, lat, lax.rem(lon + step, NLON))
     greet(barrier, near, lon)
@@ -141,7 +148,7 @@
         send[:, row, :, 0:chans] = whole.reshape(NLON, TOK, chans)
     for row in range(2):
         field[row, lon] = send[lon, row]
-    pl.semaphore_wait(barrier, NLON + greeted.astype(jnp.int32))
+    pl.semaphore_wait(barrier, NLON + NLON * greeted.astype(jnp.int32))
     pl.when(greeted)(lambda: greet(ready, far, lon))
 
     def across(step, mine):
@@ -156,6 +163,18 @@
             device_id_type=MESH,
         )
 
+    def outward(step, mine):
+        owner = lon if mine else lax.rem(lon + NLON - step, NLON)
+        there = lax.rem(lon + step, NLON)
+        return pltpu.make_async_remote_copy(
+            src_ref=send.at[there, odd],
+            dst_ref=beyond.at[owner],
+            send_sem=send_sem.at[NLON + 2 + step],
+            recv_sem=recv_sem.at[NLON + 2 + step],
+            device_id={"lat": far, "lon": there},
+            device_id_type=MESH,
+        )
+
     def onward(way, row, source, target):
         return pltpu.make_async_remote_copy(
             src_ref=edges.at[source],
@@ -171,6 +190,11 @@
 
     for step in FAR_FIRST[:-1]:
         across(step, True).start()
+
+    @pl.when(greeted)
+    def _():
+        for step in FAR_FIRST:
+            outward(step, True).start()
 
     @pl.when(jnp.logical_not(has_far))
     def _():
@@ -216,9 +240,9 @@
     edges[0] = pixels[:TOK, :EDGE].astype(BF16)
     edges[1] = pixels[TOK:, -EDGE:].astype(BF16)
 
-    @pl.when(has_far)
-    def _():
-        pl.when(greets)(lambda: pl.semaphore_wait(ready, 1))
+    @pl.when(greets)
+    def _():
+        pl.semaphore_wait(ready, 1)
         to_far.start()
 
     to_near.start()
@@ -317,7 +341,20 @@
     last_taps(second_rows(9, 6), 3)
 
     from_near.wait_recv()
-    pl.when(has_far)(lambda: from_far.wait_recv())
+    pl.when(greeted)(lambda: from_far.wait_recv())
+
+    def decode(side, lanes):
+        row = jnp.concatenate([beyond[k] for k in range(NLON)], axis=1)
+        part = dec_v[:, :, lanes].reshape(NLON * 128, EDGE)
+        halo[side] = jnp.dot(row, part, preferred_element_type=F32).astype(BF16)
+
+    @pl.when(greets)
+    def _():
+        for step in FAR_FIRST:
+            outward(step, False).wait_recv()
+        pl.when(odd == 0)(lambda: decode(0, slice(ROWL * PATCH - EDGE, ROWL * PATCH)))
+        pl.when(odd == 1)(lambda: decode(1, slice(0, EDGE)))
+
     tokens[0, :, :, -EDGE:] = halo[0].astype(F32).reshape(TQ, CG, EDGE)
     tokens[3, :, :, :EDGE] = halo[1].astype(F32).reshape(TQ, CG, EDGE)
     spread((0, 1, 2, 19, 20, 21))
@@ -329,7 +366,12 @@
     for step in FAR_FIRST[:-1]:
         across(step, True).wait_send()
     to_near.wait_send()
-    pl.when(has_far)(lambda: to_far.wait_send())
+    pl.when(greets)(lambda: to_far.wait_send())
+
+    @pl.when(greeted)
+    def _():
+        for step in FAR_FIRST:
+            outward(step, True).wait_send()
 
 
 def order_kernel(taps, order_v, result, sums):
@@ -368,6 +410,7 @@
             pltpu.VMEM((2, NLON, TOK, 128), BF16),
             pltpu.VMEM((2, TOK, EDGE), BF16),
             pltpu.VMEM((2, TOK, EDGE), BF16),
+            pltpu.VMEM((NLON, TOK, 128), BF16),
             pltpu.VMEM((NLON, 128, ROWL * PATCH), BF16),
             pltpu.VMEM((3, CH, 2 * CH), BF16),
             pltpu.VMEM((4, 3 * CH, CH), BF16),
@@ -385,8 +428,8 @@
             dma((5,)),
             dma((NLON,)),
             dma((3, 3)),
-            dma((NLON + 2,)),
-            dma((NLON + 2,)),
+            dma((2 * NLON + 2,)),
+            dma((2 * NLON + 2,)),
             pltpu.SemaphoreType.REGULAR,
         ],
         compiler_params=pltpu.CompilerParams(

time: 16.5 us -> 14.8 us (0.90); the launches traced: 16.5 us -> 14.6 us
  Pallas kernels: 16.5 us -> 14.6 us
    pallas_call x1, Pallas kernels: 15.5 us -> 13.6 us  [per_device(): pl.pallas_call(field_kernel, out_shape=(pltpu.VMEM((SECOND // 2, 8, 3 * 4...]
where the time goes in v6:
time: 14.8 us; the launch traced here: 14.6 us
  Pallas kernels  14.6 us (99%)
    pallas_call x1, Pallas kernels, per_device(): pl.pallas_call(field_kernel, out_shape=(pltpu.VMEM((SECOND // 2, 8, 3 * 4...  13.6 us
    pallas_call x1, Pallas kernels, per_device(): pl.pallas_call(order_kernel, out_shape=jax.ShapeDtypeStruct((ROWS, COLS),...  1 us

profile of v6, /device:TPU:103, one launch (start us, length us, event | category | flops | bytes accessed | tf_op | source)
XLA Modules:
  0.0 14.6 jit_solution(14590035945424254665)
XLA Ops:
  0.0 13.6 %field_to_taps.1 = (f32[9,8,1152]{2,1,0:T(8,128)S(1)}, bf16[1152,512]{1,0:T(8,128)(2,1)S(1)}) custom-call(bf16[2,90,2,96]{3,2,1,0:T(2,128)(2,1)} %modes_ref.1, bf16[384,180]{1,0:T(8,128)(2,1)} %constant.4.clone.table_ref, bf16[2,1152,512]{2,1,0:T(8,128)(2,1)} %constant.5.clone.order_ref, bf16[768,1280]{1,0:T(8,128)(2,1)} %dec_ref.1, ...), custom_call_target="tpu_custom_call" | custom-call | tf_op jit(solution)/shard_map/field_to_taps/pallas_call | solution.py:401
  13.6 1.0 %order.1 = f32[16,180]{1,0:T(8,128)} custom-call(f32[9,8,1152]{2,1,0:T(8,128)S(1)} %get-tuple-element.7.taps, bf16[1152,512]{1,0:T(8,128)(2,1)S(1)} %get-tuple-element.8.order_v), custom_call_target="tpu_custom_call" | custom-call | tf_op jit(solution)/shard_map/order/pallas_call | solution.py:454

commit v7 on v6

--- a/solution.py
+++ b/solution.py
@@ -127,13 +127,14 @@
         there = {"lat": row, "lon": column}
         pl.semaphore_signal(semaphore, inc=1, device_id=there, device_id_type=MESH)
 
+    for step in FAR_FIRST[:-1]:
+        greet(barrier, lat, lax.rem(lon + step, NLON))
+
     @pl.when(greets)
     def _():
         for step in FAR_FIRST:
             greet(barrier, far, lax.rem(lon + step, NLON))
 
-    for step in FAR_FIRST[:-1]:
-        greet(barrier, lat, lax.rem(lon + step, NLON))
     greet(barrier, near, lon)
     for copy in late + middle + last:
         copy.start()
@@ -230,13 +231,22 @@
         mid_v[2, here] = (0.5 * (ends - centre)).astype(BF16)
     for copy in last[:NLON]:
         copy.wait()
-    for step in FAR_FIRST[:-1]:
-        across(step, False).wait_recv()
     top, bottom = lat == 0, lat == nlat - 1
-    weights = dec_v[...].reshape(NLON * 128, ROWL * PATCH)
-
-    values = jnp.concatenate([field[:, k].reshape(2 * TOK, 128) for k in range(NLON)], axis=1)
-    pixels = jnp.dot(values, weights, preferred_element_type=F32)
+    pixels = None
+    for group in ((0, 4), (3, 5), (1, 7), (2, 6)):
+        rows, weights = [], []
+        for step in group:
+            if step:
+                across(step, False).wait_recv()
+            origin = lax.rem(lon + NLON - step, NLON)
+            rows.append(field[:, origin].reshape(2 * TOK, 128))
+            weights.append(dec_v[origin])
+        part = jnp.dot(
+            jnp.concatenate(rows, axis=1),
+            jnp.concatenate(weights, axis=0),
+            preferred_element_type=F32,
+        )
+        pixels = part if pixels is None else pixels + part
     edges[0] = pixels[:TOK, :EDGE].astype(BF16)
     edges[1] = pixels[TOK:, -EDGE:].astype(BF16)
 
@@ -303,10 +313,15 @@
                 first[2, here] = (left[1:] - right[:-1]).reshape(STEP, CH).astype(BF16)
                 first[3, here] = (right[:-1] - right[1:]).reshape(STEP, CH).astype(BF16)
 
-    def second_rows(low, count):
+    def second_rows(*spans):
+        order = [i for low, high in spans for i in range(low, high)]
+        count = len(order)
         products = []
         for k in range(4):
-            blocks = [first[k, (low + a) * STEP : (low + a + count) * STEP] for a in range(3)]
+            blocks = []
+            for a in range(3):
+                parts = [first[k, (low + a) * STEP : (high + a) * STEP] for low, high in spans]
+                blocks.append(jnp.concatenate(parts, axis=0))
             products.append(
                 jnp.dot(jnp.concatenate(blocks, axis=1), mid_v[k], preferred_element_type=F32)
             )
@@ -316,29 +331,29 @@
         )
         pair = [jnp.maximum(x, 0.0).reshape(count, STEP, CH) for x in pair]
         rows = []
-        for step in range(count):
+        for step, i in enumerate(order):
             values = [x[step] for x in pair]
-            if low + step == 0:
+            if i == 0:
                 values = [jnp.where(top, 0.0, x) for x in values]
-            if low + step == SECOND - 1:
+            if i == SECOND - 1:
                 values = [jnp.where(bottom, 0.0, x) for x in values]
             rows += [x.astype(BF16) for x in values]
         return rows
 
     def last_taps(rows, slot):
-        for i in range(0, len(rows), 4):
-            tap = lax.dot_general(
-                out_v[...],
-                jnp.concatenate(rows[i : i + 4], axis=0),
-                (((1,), (1,)), ((), ())),
-                preferred_element_type=F32,
-            )
-            taps[slot + i // 4] = jnp.concatenate([tap[b * 8 : b * 8 + 8] for b in range(3)], axis=1)
+        tap = lax.dot_general(
+            out_v[...],
+            jnp.concatenate(rows, axis=0),
+            (((1,), (1,)), ((), ())),
+            preferred_element_type=F32,
+        )
+        for i in range(len(rows) // 4):
+            part = tap[:, i * 4 * STEP : (i + 1) * 4 * STEP]
+            taps[slot + i] = jnp.concatenate([part[b * 8 : b * 8 + 8] for b in range(3)], axis=1)
 
     spread(range(3, 19))
     first_rows(range(3, 17))
-    last_taps(second_rows(3, 6), 0)
-    last_taps(second_rows(9, 6), 3)
+    last_taps(second_rows((3, 15)), 0)
 
     from_near.wait_recv()
     pl.when(greeted)(lambda: from_far.wait_recv())
@@ -359,7 +374,7 @@
     tokens[3, :, :, :EDGE] = halo[1].astype(F32).reshape(TQ, CG, EDGE)
     spread((0, 1, 2, 19, 20, 21))
     first_rows((0, 1, 2, 17, 18, 19))
-    last_taps(second_rows(0, 3) + second_rows(15, 3), 6)
+    last_taps(second_rows((0, 3), (15, 18)), 6)
 
     for copy in last[NLON:]:
         copy.wait()

time: 14.8 us -> 14.7 us (level)
  Pallas kernels: 14.6 us -> 14.4 us
    pallas_call x1, Pallas kernels: 13.6 us -> 13.4 us  [per_device(): pl.pallas_call(field_kernel, out_shape=(pltpu.VMEM((SECOND // 2, 8, 3 * 4...]
where the time goes in v7:
time: 14.7 us; the launch traced here: 14.4 us
  Pallas kernels  14.4 us (98%)
    pallas_call x1, Pallas kernels, per_device(): pl.pallas_call(field_kernel, out_shape=(pltpu.VMEM((SECOND // 2, 8, 3 * 4...  13.4 us
    pallas_call x1, Pallas kernels, per_device(): pl.pallas_call(order_kernel, out_shape=jax.ShapeDtypeStruct((ROWS, COLS),...  1 us

profile of v7, /device:TPU:103, one launch (start us, length us, event | category | flops | bytes accessed | tf_op | source)
XLA Modules:
  0.0 14.4 jit_solution(14612688084102097956)
XLA Ops:
  0.0 13.4 %field_to_taps.1 = (f32[9,8,1152]{2,1,0:T(8,128)S(1)}, bf16[1152,512]{1,0:T(8,128)(2,1)S(1)}) custom-call(bf16[2,90,2,96]{3,2,1,0:T(2,128)(2,1)} %modes_ref.1, bf16[384,180]{1,0:T(8,128)(2,1)} %constant.4.clone.table_ref, bf16[2,1152,512]{2,1,0:T(8,128)(2,1)} %constant.5.clone.order_ref, bf16[768,1280]{1,0:T(8,128)(2,1)} %dec_ref.1, ...), custom_call_target="tpu_custom_call" | custom-call | tf_op jit(solution)/shard_map/field_to_taps/pallas_call | solution.py:416
  13.4 1.0 %order.1 = f32[16,180]{1,0:T(8,128)} custom-call(f32[9,8,1152]{2,1,0:T(8,128)S(1)} %get-tuple-element.7.taps, bf16[1152,512]{1,0:T(8,128)(2,1)S(1)} %get-tuple-element.8.order_v), custom_call_target="tpu_custom_call" | custom-call | tf_op jit(solution)/shard_map/order/pallas_call | solution.py:469

commit v8 on v7

--- a/solution.py
+++ b/solution.py
@@ -109,8 +109,6 @@
     ] + [
         pltpu.make_async_copy(order_ref.at[lax.rem(lon, 2)], order_v, local_sem.at[4]),
     ]
-    for copy in early:
-        copy.start()
     barrier = pltpu.get_barrier_semaphore()
 
     odd = lax.rem(lat, 2)
@@ -127,15 +125,17 @@
         there = {"lat": row, "lon": column}
         pl.semaphore_signal(semaphore, inc=1, device_id=there, device_id_type=MESH)
 
+    @pl.when(greets)
+    def _():
+        for step in FAR_FIRST:
+            greet(barrier, far, lax.rem(lon + step, NLON))
+
     for step in FAR_FIRST[:-1]:
         greet(barrier, lat, lax.rem(lon + step, NLON))
 
-    @pl.when(greets)
-    def _():
-        for step in FAR_FIRST:
-            greet(barrier, far, lax.rem(lon + step, NLON))
-
     greet(barrier, near, lon)
+    for copy in early:
+        copy.start()
     for copy in late + middle + last:
         copy.start()
     send[...] = jnp.zeros_like(send)
@@ -250,11 +250,6 @@
     edges[0] = pixels[:TOK, :EDGE].astype(BF16)
     edges[1] = pixels[TOK:, -EDGE:].astype(BF16)
 
-    @pl.when(greets)
-    def _():
-        pl.semaphore_wait(ready, 1)
-        to_far.start()
-
     to_near.start()
     tokens[1:3] = pixels.reshape(2, TQ, CG, ROWL * PATCH)
 
@@ -353,6 +348,12 @@
 
     spread(range(3, 19))
     first_rows(range(3, 17))
+
+    @pl.when(greets)
+    def _():
+        pl.semaphore_wait(ready, 1)
+        to_far.start()
+
     last_taps(second_rows((3, 15)), 0)
 
     from_near.wait_recv()

time: 14.7 us -> 15.2 us (1.034)
  the two profiles are of different devices: /device:TPU:103 before, /device:TPU:167 now
where the time goes in v8:
time: 15.2 us; the launch traced here: 15.1 us
  Pallas kernels  15.1 us (99%)
    pallas_call x1, Pallas kernels, per_device(): pl.pallas_call(field_kernel, out_shape=(pltpu.VMEM((SECOND // 2, 8, 3 * 4...  14.1 us
    pallas_call x1, Pallas kernels, per_device(): pl.pallas_call(order_kernel, out_shape=jax.ShapeDtypeStruct((ROWS, COLS),...  1.01 us

profile of v8, /device:TPU:167, one launch (start us, length us, event | category | flops | bytes accessed | tf_op | source)
XLA Modules:
  0.0 15.1 jit_solution(16365539801680877396)
XLA Ops:
  0.0 14.1 %field_to_taps.1 = (f32[9,8,1152]{2,1,0:T(8,128)S(1)}, bf16[1152,512]{1,0:T(8,128)(2,1)S(1)}) custom-call(bf16[2,90,2,96]{3,2,1,0:T(2,128)(2,1)} %modes_ref.1, bf16[384,180]{1,0:T(8,128)(2,1)} %constant.4.clone.table_ref, bf16[2,1152,512]{2,1,0:T(8,128)(2,1)} %constant.5.clone.order_ref, bf16[768,1280]{1,0:T(8,128)(2,1)} %dec_ref.1, ...), custom_call_target="tpu_custom_call" | custom-call | tf_op jit(solution)/shard_map/field_to_taps/pallas_call | solution.py:417
  14.1 1.0 %order.1 = f32[16,180]{1,0:T(8,128)} custom-call(f32[9,8,1152]{2,1,0:T(8,128)S(1)} %get-tuple-element.7.taps, bf16[1152,512]{1,0:T(8,128)(2,1)S(1)} %get-tuple-element.8.order_v), custom_call_target="tpu_custom_call" | custom-call | tf_op jit(solution)/shard_map/order/pallas_call | solution.py:470

commit v9 on v8

--- a/solution.py
+++ b/solution.py
@@ -109,6 +109,8 @@
     ] + [
         pltpu.make_async_copy(order_ref.at[lax.rem(lon, 2)], order_v, local_sem.at[4]),
     ]
+    for copy in early:
+        copy.start()
     barrier = pltpu.get_barrier_semaphore()
 
     odd = lax.rem(lat, 2)
@@ -125,17 +127,15 @@
         there = {"lat": row, "lon": column}
         pl.semaphore_signal(semaphore, inc=1, device_id=there, device_id_type=MESH)
 
+    for step in FAR_FIRST[:-1]:
+        greet(barrier, lat, lax.rem(lon + step, NLON))
+
     @pl.when(greets)
     def _():
         for step in FAR_FIRST:
             greet(barrier, far, lax.rem(lon + step, NLON))
 
-    for step in FAR_FIRST[:-1]:
-        greet(barrier, lat, lax.rem(lon + step, NLON))
-
     greet(barrier, near, lon)
-    for copy in early:
-        copy.start()
     for copy in late + middle + last:
         copy.start()
     send[...] = jnp.zeros_like(send)

time: 15.2 us -> 15.2 us (level)
  the two profiles are of different devices: /device:TPU:167 before, /device:TPU:135 now
where the time goes in v9:
time: 15.2 us; the launch traced here: 15.1 us
  Pallas kernels  15.1 us (99%)
    pallas_call x1, Pallas kernels, per_device(): pl.pallas_call(field_kernel, out_shape=(pltpu.VMEM((SECOND // 2, 8, 3 * 4...  14.1 us
    pallas_call x1, Pallas kernels, per_device(): pl.pallas_call(order_kernel, out_shape=jax.ShapeDtypeStruct((ROWS, COLS),...  1.01 us

profile of v9, /device:TPU:135, one launch (start us, length us, event | category | flops | bytes accessed | tf_op | source)
XLA Modules:
  0.0 15.1 jit_solution(3962835271832983375)
XLA Ops:
  0.0 14.1 %field_to_taps.1 = (f32[9,8,1152]{2,1,0:T(8,128)S(1)}, bf16[1152,512]{1,0:T(8,128)(2,1)S(1)}) custom-call(bf16[2,90,2,96]{3,2,1,0:T(2,128)(2,1)} %modes_ref.1, bf16[384,180]{1,0:T(8,128)(2,1)} %constant.4.clone.table_ref, bf16[2,1152,512]{2,1,0:T(8,128)(2,1)} %constant.5.clone.order_ref, bf16[768,1280]{1,0:T(8,128)(2,1)} %dec_ref.1, ...), custom_call_target="tpu_custom_call" | custom-call | tf_op jit(solution)/shard_map/field_to_taps/pallas_call | solution.py:417
  14.1 1.0 %order.1 = f32[16,180]{1,0:T(8,128)} custom-call(f32[9,8,1152]{2,1,0:T(8,128)S(1)} %get-tuple-element.7.taps, bf16[1152,512]{1,0:T(8,128)(2,1)S(1)} %get-tuple-element.8.order_v), custom_call_target="tpu_custom_call" | custom-call | tf_op jit(solution)/shard_map/order/pallas_call | solution.py:470
